TPU v7x, 256 devices: a whole 4x4x8 slice. The times are simulated.
256 devices in a mesh: row: 16 (over y, z_hi), col: 16 (over z_lo, x, core).
Axes of the slice: x: 4, y: 4, z: 8 (z_hi: 4, z_lo: 2; z = z_hi * 2 + z_lo), core: 2. Of those that a mesh axis runs over, the one named last changes fastest.
Arguments:
- tokens_in: bfloat16 [1024, 12288], P('col', 'row'), may hold values from -6 to 6
- weight_up: bfloat16 [12288, 49152], P('row', 'col'), may hold values from -0.0546875 to 0.0546875
- bias_up: float32 [49152], P('col'), may hold values from -4 to 4
- cotangent: bfloat16 [1024, 49152], P('row', 'col'), may hold values from -0.59765625 to 0.59765625
Outputs:
- activated: bfloat16 [1024, 49152], P('row', 'col')
- grad_tokens: bfloat16 [1024, 12288], P('col', 'row')
- grad_weight: bfloat16 [12288, 49152], P('row', 'col')
- grad_bias: float32 [49152], P('col')
All inputs are finite; a program needn't handle non-finite values.
Results may differ from a plain program's by a relative error of at most 0.027.
Values may be sent and summed in bfloat16 or wider, within the bound.
A program may use at most 128 MiB of HBM per device.

v0:
```python
import jax
import jax.numpy as jnp
from jax import lax
from jax.sharding import PartitionSpec as P


def gelu_tanh(values):
    return jax.nn.gelu(values, approximate=True)


def on_device(tokens_in, weight_up, bias_up, cotangent):
    gathered = lax.all_gather(tokens_in, "col", axis=0, tiled=True)
    block = gathered
    hidden = (
        lax.psum_scatter(
            jnp.dot(block, weight_up, preferred_element_type=jnp.float32).astype(jnp.bfloat16),
            "row",
            scatter_dimension=0,
            tiled=True,
        ).astype(jnp.float32)
        + bias_up
    )
    outputs, pullback = jax.vjp(gelu_tanh, hidden)
    activated = outputs.astype(jnp.bfloat16)
    local_grad = pullback(cotangent.astype(jnp.float32))[0].astype(jnp.bfloat16)
    grad_hidden = lax.all_gather(local_grad, "row", axis=0, tiled=True)
    grad_bias = jnp.sum(grad_hidden, axis=0, dtype=jnp.float32)
    grad_weight = lax.dot_general(
        gathered, grad_hidden, (((0,), (0,)), ((), ())), preferred_element_type=jnp.float32
    ).astype(jnp.bfloat16)
    block = grad_hidden
    grad_tokens = lax.psum_scatter(
        lax.dot_general(
            block, weight_up, (((1,), (1,)), ((), ())), preferred_element_type=jnp.float32
        ).astype(jnp.bfloat16),
        "col",
        scatter_dimension=0,
        tiled=True,
    )
    return (activated, grad_tokens, grad_weight, grad_bias)


def solution(mesh):
    return jax.shard_map(
        on_device,
        mesh=mesh,
        in_specs=(P("col", "row"), P("row", "col"), P("col"), P("row", "col")),
        out_specs=(P("row", "col"), P("col", "row"), P("row", "col"), P("col")),
        check_vma=False,
    )
```

profile of v0, /device:TPU:2, one launch (start us, length us, event | category | flops | bytes accessed | tf_op | source)
XLA Modules:
  0.0 341.3 jit_solution(18133822557197474019)
XLA Ops:
  7.2 0.0 all-gather.3.cloned.1.call-start
  7.2 0.7 all-gather.3.cloned.1.call-update
  7.9 0.0 reduce-scatter.3.cloned.1.call-start
  7.9 40.3 %all-gather.3.cloned.1.call-done = bf16[1024,768]{1,0:T(8,128)(2,1)} async-done(((bf16[64,768]{1,0:T(8,128)(2,1)}), bf16[1024,768]{1,0:T(8,128)(2,1)}) %all-gather.3.cloned.1.call-update) | async-done | bytes 1572880 | tf_op jit(solution)/shard_map/all_gather | solution.py:12
  48.2 9.1 %convolution_convert_fusion = bf16[1024,3072]{1,0:T(8,128)(2,1)} fusion(bf16[1024,768]{1,0:T(8,128)(2,1)} %all-gather.3.cloned.1.call-done, bf16[768,3072]{1,0:T(8,128)(2,1)} %param.5), kind=kOutput, calls=%fused_computation.1 | convolution fusion | flops 4834983936 | bytes 12582912 | tf_op jit(solution)/shard_map/dot_general | solution.py:16
  57.4 0.0 copy-start
  57.4 0.0 copy-start.1
  57.4 0.0 reduce-scatter.3.cloned.1.call-update
  57.4 0.0 all-gather.5.cloned.1.call-start
  57.4 109.4 %reduce-scatter.3.cloned.1.call-done = bf16[64,3072]{1,0:T(8,128)(2,1)} async-done(((bf16[1024,3072]{1,0:T(8,128)(2,1)}), bf16[64,3072]{1,0:T(8,128)(2,1)}) %reduce-scatter.3.cloned.1.call-update) | async-done | bytes 393232 | tf_op jit(solution)/shard_map/reduce_scatter | solution.py:15
  166.8 0.0 copy-done
  166.8 0.0 copy-done.1
  166.8 2.5 fusion.3
  169.3 0.0 all-gather.5.cloned.1.call-update
  169.4 0.0 copy-start.2
  169.4 0.0 reduce-scatter.5.cloned.1.call-start
  169.4 96.3 %all-gather.5.cloned.1.call-done = bf16[1024,3072]{1,0:T(8,128)(2,1)} async-done(((bf16[64,3072]{1,0:T(8,128)(2,1)}), bf16[1024,3072]{1,0:T(8,128)(2,1)}) %all-gather.5.cloned.1.call-update) | async-done | bytes 6291472 | tf_op jit(solution)/shard_map/all_gather | solution.py:26
  265.8 9.5 %convolution_convert_fusion.2 = bf16[1024,768]{1,0:T(8,128)(2,1)} fusion(bf16[1024,3072]{1,0:T(8,128)(2,1)} %all-gather.5.cloned.1.call-done, bf16[768,3072]{1,0:T(8,128)(2,1)} %param.5), kind=kOutput, calls=%fused_computation.4 | convolution fusion | flops 4832624640 | bytes 12582912 | tf_op jit(solution)/shard_map/dot_general | solution.py:33
  275.3 0.0 reduce-scatter.5.cloned.1.call-update
  275.3 0.0 copy-done.2
  275.3 9.8 %fusion = bf16[768,3072]{0,1:T(8,128)(2,1)} fusion(bf16[1024,3072]{1,0:T(8,128)(2,1)} %all-gather.5.cloned.1.call-done, bf16[1024,768]{1,0:T(8,128)(2,1)S(1)} %copy-done.2), kind=kOutput, calls=%fused_computation.3 | convolution fusion | flops 4834197504 | bytes 12582912 | tf_op jit(solution)/shard_map/dot_general | solution.py:28
  285.1 6.6 %copy.8 = bf16[768,3072]{1,0:T(8,128)(2,1)} copy(bf16[768,3072]{0,1:T(8,128)(2,1)} %fusion) | data formatting | bytes 9437184
  291.8 4.3 %convert_reduce_fusion = f32[3072]{0:T(1024)} fusion(bf16[1024,3072]{1,0:T(8,128)(2,1)} %all-gather.5.cloned.1.call-done), kind=kLoop, calls=%fused_computation | loop fusion | flops 6288384 | bytes 6303744 | tf_op jit(solution)/shard_map/reduce_sum | solution.py:27
  296.1 38.7 %reduce-scatter.5.cloned.1.call-done = bf16[64,768]{1,0:T(8,128)(2,1)} async-done(((bf16[1024,768]{1,0:T(8,128)(2,1)}), bf16[64,768]{1,0:T(8,128)(2,1)}) %reduce-scatter.5.cloned.1.call-update) | async-done | bytes 98320 | tf_op jit(solution)/shard_map/reduce_scatter | solution.py:32
Async XLA Ops:
  7.2 41.1 %all-gather.3.cloned.1.call-start = ((), (), s32[]{:S(2)}) async-start(), calls=%async_computation.2 | async-start | bytes 1671168 | tf_op jit(solution)/shard_map/all_gather | solution.py:12
  7.9 158.9 %reduce-scatter.3.cloned.1.call-start = ((), (), s32[]{:S(2)}) async-start(), calls=%async_computation.3 | async-start | bytes 6684672 | tf_op jit(solution)/shard_map/reduce_scatter | solution.py:15
  57.4 109.5 %copy-start = (bf16[64,3072]{1,0:T(8,128)(2,1)S(1)}, bf16[64,3072]{1,0:T(8,128)(2,1)}, u32[]{:S(2)}) copy-start(bf16[64,3072]{1,0:T(8,128)(2,1)} %param.7) | copy-start | bytes 1179652
  57.4 109.5 %copy-start.1 = (f32[3072]{0:T(1024)S(1)}, f32[3072]{0:T(1024)}, u32[]{:S(2)}) copy-start(f32[3072]{0:T(1024)} %param.6) | copy-start | bytes 36868
  57.4 208.4 %all-gather.5.cloned.1.call-start = ((), (), s32[]{:S(2)}) async-start(), calls=%async_computation.4 | async-start | bytes 6684672 | tf_op jit(solution)/shard_map/all_gather | solution.py:26
  169.4 105.9 %copy-start.2 = (bf16[1024,768]{1,0:T(8,128)(2,1)S(1)}, bf16[1024,768]{1,0:T(8,128)(2,1)}, u32[]{:S(2)}) copy-start(bf16[1024,768]{1,0:T(8,128)(2,1)} %all-gather.3.cloned.1.call-done) | copy-start | bytes 4718596
  169.4 165.4 %reduce-scatter.5.cloned.1.call-start = ((), (), s32[]{:S(2)}) async-start(), calls=%async_computation.5 | async-start | bytes 1671168 | tf_op jit(solution)/shard_map/reduce_scatter | solution.py:32
Sparse Core Ops, SparseCore 0:
  9.8 38.3 all-gather.2
  57.5 109.2 reduce-scatter.2
  169.9 95.8 all-gather.4
  275.4 59.3 reduce-scatter.4
where the time goes:
time: 346 us; the launch traced here: 341 us
  waiting for transfers between devices  285 us (82%)
  matrix products  28.4 us (8%)
  between operations  13.8 us (4%)
  other arithmetic  6.83 us (2%)
  local copies, waits for them, and re-layouts  6.64 us (2%)
    reduce_scatter x1, waiting for transfers between devices, on_device(): lax.psum_scatter(jnp.dot(block, weight_up, preferred_element_type=jnp.flo...  109 us
    all_gather x1, waiting for transfers between devices, on_device(): grad_hidden = lax.all_gather(local_grad, 'row', axis=0, tiled=True)  96.3 us
    all_gather x1, waiting for transfers between devices, on_device(): gathered = lax.all_gather(tokens_in, 'col', axis=0, tiled=True)  40.3 us
    reduce_scatter x1, waiting for transfers between devices, on_device(): lax.psum_scatter(lax.dot_general(block, weight_up, (((1,), (1,)), ((), ()...  38.7 us
    dot_general x1, matrix products, on_device(): lax.dot_general(gathered, grad_hidden, (((0,), (0,)), ((), ())), preferre...  9.82 us
    dot_general x1, matrix products, on_device(): lax.dot_general(block, weight_up, (((1,), (1,)), ((), ())), preferred_ele...  9.49 us
    dot_general x1, matrix products, on_device(): jnp.dot(block, weight_up, preferred_element_type=jnp.float32)  9.12 us
  transfers between devices with their start and end apart: 4, of which 4 were waited for; matrix products, arithmetic and copies ran while one was open for 6% of the time, Pallas kernels for 0%

commit v1 on v0

v1 whole, which is shorter than its diff:
```python
import functools

import jax
import jax.numpy as jnp
from jax import lax
from jax.experimental import pallas as pl
from jax.experimental.pallas import tpu as pltpu
from jax.sharding import PartitionSpec as P

MESH = pl.DeviceIdType.MESH
BF16 = jnp.bfloat16
F32 = jnp.float32
TOK, DB, FB, BLK = 1024, 768, 3072, 64
KINDS = ("z", "y", "y", "y", "y", "y")
J = len(KINDS)
W = FB // J
GELU_C = 0.7978845608028654
GELU_A = 0.044715


def schedule():
    order = []
    for t in range(J + 5):
        for step, lag in (("F1", 0), ("F2", 0), ("F5", 1), ("F6", 2), ("F3", 0), ("F7", 2), ("F8", 3), ("F9", 4)):
            if 0 <= t - lag < J:
                order.append((step, t - lag))
    return order


def kernel(
    tok_in, w_in, b_in, cot_in, act_out, gt_out, gw_out, gb_out,
    tok, tokt, wv, cot, bias, part, ra, rb, mine, zs, zr, zo, gh, act, gw, gb, gtacc, gts, gpr, gx, gxr, gto,
    lsem, ssem, rsem,
):
    row, col = lax.axis_index("row"), lax.axis_index("col")
    y, zh = row // 4, row % 4
    q, core = col // 2, col % 2
    other = 1 - core

    sends, used = [], {"r": 0, "l": 0}

    def remote(src, dst, device):
        i = used["r"]
        used["r"] += 1
        copy = pltpu.make_async_remote_copy(
            src_ref=src, dst_ref=dst, send_sem=ssem.at[i], recv_sem=rsem.at[i], device_id=device, device_id_type=MESH
        )
        copy.start()
        sends.append(copy)
        return copy

    def local(src, dst):
        i = used["l"]
        used["l"] += 1
        copy = pltpu.make_async_copy(src, dst, lsem.at[i])
        copy.start()
        return copy

    partner = (row, q * 2 + other)

    def chip(d):
        return lax.rem(q + d, 8)

    own_tok = local(tok_in, tok.at[col // 4, col % 4])
    w_loads = [local(w_in.at[:, pl.ds(j * W, W)], wv.at[j]) for j in range(J)]
    cot_load = local(cot_in, cot)
    bias_load = local(b_in, bias)

    barrier = pltpu.get_barrier_semaphore()
    peers = [(lax.rem(row + 4 * d, 16), col) for d in (1, 2, 3)]
    peers += [(y * 4 + lax.rem(zh + d, 4), col) for d in (1, 2, 3)]
    peers += [(row, chip(d) * 2 + core) for d in range(1, 8)] + [partner]
    for peer in peers:
        pl.semaphore_signal(barrier, inc=1, device_id=peer, device_id_type=MESH)
    pl.semaphore_wait(barrier, len(peers))

    direct = [remote(tok_in, tok.at[col // 4, col % 4], (row, chip(d) * 2 + core)) for d in range(1, 8)]
    passed = [remote(tok_in, tok.at[col // 4, col % 4], partner)]
    for d in range(1, 8):
        direct[d - 1].wait_recv()
        k = chip(8 - d) * 2 + core
        passed.append(remote(tok.at[k // 4, k % 4], tok.at[k // 4, k % 4], partner))
    for copy in passed:
        copy.wait_recv()
    own_tok.wait()

    def geometry(j):
        return (y, zh, 4, 1) if KINDS[j] == "y" else (zh, y, 1, 4)

    def near(i, d):
        return lax.rem(i + 4 + d, 4)

    def block(j, p, s):
        _, _, pm, sm = geometry(j)
        return p * pm + s * sm

    def product(j, p):
        left = tok[p] if KINDS[j] == "y" else tok[:, p]
        return jnp.dot(left.reshape(4 * BLK, DB), wv[j], preferred_element_type=F32).reshape(4, BLK, W)

    done = {}

    def f1(j):
        p, s, _, _ = geometry(j)
        w_loads[j].wait()
        p2 = near(p, 2)
        part[j, p2] = product(j, p2).astype(BF16)
        done["a", j] = [
            remote(part.at[j, p2, pl.ds(0, 2)], ra.at[j, 0], (block(j, near(p, 1), s), col)),
            remote(part.at[j, p2, pl.ds(2, 2)], ra.at[j, 1], (block(j, near(p, -1), s), col)),
        ]

    def f2(j):
        p, s, _, _ = geometry(j)
        up, down = near(p, 1), near(p, -1)
        part[j, up] = product(j, up).astype(BF16)
        done["b", j] = [remote(part.at[j, up, pl.ds(2, 2)], rb.at[j, 0, pl.ds(2, 2)], (block(j, up, s), col))]
        part[j, down] = product(j, down).astype(BF16)
        done["b", j] += [remote(part.at[j, down, pl.ds(0, 2)], rb.at[j, 1, pl.ds(0, 2)], (block(j, down, s), col))]

    def f3(j):
        p, s, _, _ = geometry(j)
        up, down = near(p, 1), near(p, -1)
        for i, (to, at) in enumerate(((up, 0), (down, 2))):
            done["a", j][i].wait_recv()
            part[j, to, pl.ds(at, 2)] = (part[j, to, pl.ds(at, 2)].astype(F32) + ra[j, i].astype(F32)).astype(BF16)
            done["b", j] += [remote(part.at[j, to, pl.ds(at, 2)], rb.at[j, i, pl.ds(at, 2)], (block(j, to, s), col))]

    def f5(j):
        p, s, _, _ = geometry(j)
        mine[...] = product(j, p)
        for copy in done["b", j]:
            copy.wait_recv()

        def total(t):
            return mine[t] + rb[j, 0, t].astype(F32) + rb[j, 1, t].astype(F32)

        done["z", j] = []
        for d in (2, 1, 3):
            t = near(s, d)
            zs[j, d - 1] = total(t).astype(BF16)
            done["z", j] += [remote(zs.at[j, d - 1], zr.at[j, d - 1], (block(j, p, t), col))]
        zo[j] = total(s)

    def f6(j):
        p, s, _, _ = geometry(j)
        k = block(j, p, s)
        columns = pl.ds(j * W, W)
        for copy in done["z", j]:
            copy.wait_recv()
        hidden = zo[j] + zr[j, 0].astype(F32) + zr[j, 1].astype(F32) + zr[j, 2].astype(F32) + bias[:, columns]
        square = hidden * hidden
        tanh = jnp.tanh(GELU_C * hidden * (1.0 + GELU_A * square))
        half = 0.5 * (1.0 + tanh)
        act[j] = (hidden * half).astype(BF16)
        slope = half + 0.5 * hidden * (1.0 - tanh * tanh) * (GELU_C * (1.0 + 3.0 * GELU_A * square))
        gh[j, y, zh] = (cot[:, columns].astype(F32) * slope).astype(BF16)
        mineref = gh.at[j, y, zh]
        done["g", j] = [remote(mineref, mineref, (block(j, p, near(s, d)), col)) for d in (1, 2, 3)]
        done["up", j] = [remote(mineref, mineref, (block(j, near(p, 1), s), col))]
        done["down", j] = [remote(mineref, mineref, (block(j, near(p, -1), s), col))]
        done["act", j] = local(act.at[j], act_out.at[:, columns])

    def f7(j):
        p, s, _, _ = geometry(j)
        for d in (1, 2, 3):
            done["g", j][d - 1].wait_recv()
            k = block(j, p, near(s, -d))
            ref = gh.at[j, k // 4, k % 4]
            done["up", j] += [remote(ref, ref, (block(j, near(p, 1), s), col))]
            done["down", j] += [remote(ref, ref, (block(j, near(p, -1), s), col))]

    def f8(j):
        p, s, _, _ = geometry(j)
        done["far", j] = []
        for d in (0, 1):
            done["up", j][d].wait_recv()
            k = block(j, near(p, -1), near(s, -d))
            ref = gh.at[j, k // 4, k % 4]
            done["far", j] += [remote(ref, ref, (block(j, near(p, 1), s), col))]
        for d in (2, 3):
            done["down", j][d].wait_recv()
            k = block(j, near(p, 1), near(s, -d))
            ref = gh.at[j, k // 4, k % 4]
            done["far", j] += [remote(ref, ref, (block(j, near(p, -1), s), col))]

    def f9(j):
        for d in (0, 1):
            done["down", j][d].wait_recv()
        for d in (2, 3):
            done["up", j][d].wait_recv()
        for copy in done["far", j]:
            copy.wait_recv()
        columns = pl.ds(j * W, W)

        @pl.loop(0, 3)
        def _(i):
            rows = pl.ds(pl.multiple_of(i * 256, 256), 256)
            gw[j, rows] = jnp.dot(tokt[rows], gh[j].reshape(TOK, W), preferred_element_type=F32).astype(BF16)

        done["gw", j] = local(gw.at[j], gw_out.at[:, columns])
        gb[:, columns] = jnp.sum(gh[j].reshape(TOK, W).astype(F32), axis=0, keepdims=True)

        @pl.loop(0, 4)
        def _(i):
            term = lax.dot_general(
                gh[j, i].reshape(4 * BLK, W), wv[j], (((1,), (1,)), ((), ())), preferred_element_type=F32
            ).reshape(4, BLK, DB)
            if j == 0:
                gtacc[i] = term
            else:
                gtacc[i] += term

    steps = dict(F1=f1, F2=f2, F3=f3, F5=f5, F6=f6, F7=f7, F8=f8, F9=f9)
    for step, j in schedule():
        if (step, j) == ("F6", 0):
            cot_load.wait()
            bias_load.wait()
        if (step, j) == ("F9", 0):

            @pl.loop(0, 4)
            def _(i):
                tokt[:, pl.ds(pl.multiple_of(i * 256, 256), 256)] = tok[i].reshape(4 * BLK, DB).T

        steps[step](j)

    @pl.loop(0, 8)
    def _(i):
        k = i * 2 + other
        gts[i] = gtacc[k // 4, k % 4].astype(BF16)

    pair = remote(gts, gpr, partner)
    pair.wait_recv()
    over = []
    for d in range(1, 8):
        i = chip(d)
        k = i * 2 + core
        gx[d - 1] = (gtacc[k // 4, k % 4] + gpr[i].astype(F32)).astype(BF16)
        over.append(remote(gx.at[d - 1], gxr.at[d - 1], (row, k)))
    total = gtacc[col // 4, col % 4] + gpr[q].astype(F32)
    for d in range(1, 8):
        over[d - 1].wait_recv()
        total += gxr[d - 1].astype(F32)
    gto[...] = total.astype(BF16)
    last = [local(gto, gt_out), local(gb, gb_out)]

    for copy in last:
        copy.wait()
    for j in range(J):
        done["act", j].wait()
        done["gw", j].wait()
    for copy in sends:
        copy.wait_send()


def on_device(tokens_in, weight_up, bias_up, cotangent):
    anywhere = pl.BlockSpec(memory_space=pl.ANY)
    v = pltpu.VMEM
    act, gt, gw, gb = pl.pallas_call(
        kernel,
        out_shape=[
            jax.ShapeDtypeStruct((BLK, FB), BF16),
            jax.ShapeDtypeStruct((BLK, DB), BF16),
            jax.ShapeDtypeStruct((DB, FB), BF16),
            jax.ShapeDtypeStruct((1, FB), F32),
        ],
        in_specs=[anywhere] * 4,
        out_specs=[anywhere] * 4,
        scratch_shapes=[
            v((4, 4, BLK, DB), BF16),
            v((DB, TOK), BF16),
            v((J, DB, W), BF16),
            v((BLK, FB), BF16),
            v((1, FB), F32),
            v((J, 4, 4, BLK, W), BF16),
            v((J, 2, 2, BLK, W), BF16),
            v((J, 2, 4, BLK, W), BF16),
            v((4, BLK, W), F32),
            v((J, 3, BLK, W), BF16),
            v((J, 3, BLK, W), BF16),
            v((J, BLK, W), F32),
            v((J, 4, 4, BLK, W), BF16),
            v((J, BLK, W), BF16),
            v((J, DB, W), BF16),
            v((1, FB), F32),
            v((4, 4, BLK, DB), F32),
            v((8, BLK, DB), BF16),
            v((8, BLK, DB), BF16),
            v((7, BLK, DB), BF16),
            v((7, BLK, DB), BF16),
            v((BLK, DB), BF16),
            pltpu.SemaphoreType.DMA((3 * J + 8,)),
            pltpu.SemaphoreType.DMA((24 * J + 24,)),
            pltpu.SemaphoreType.DMA((24 * J + 24,)),
        ],
        compiler_params=pltpu.CompilerParams(collective_id=0, has_side_effects=True, vmem_limit_bytes=60 * 2**20),
        name="updown",
    )(tokens_in, weight_up, bias_up.reshape(1, FB), cotangent)
    return act, gt, gw, gb.reshape(FB)


def solution(mesh):
    return jax.shard_map(
        on_device,
        mesh=mesh,
        in_specs=(P("col", "row"), P("row", "col"), P("col"), P("row", "col")),
        out_specs=(P("row", "col"), P("col", "row"), P("row", "col"), P("col")),
        check_vma=False,
    )
```

time: 346 us -> 183 us (0.53)
  the two profiles are of different devices: /device:TPU:2 before, /device:TPU:39 now
where the time goes in v1:
time: 183 us
  Pallas kernels  174 us (95%)
  local copies, waits for them, and re-layouts  8.77 us (5%)
    pallas_call x1, Pallas kernels, on_device(): pl.pallas_call(kernel, out_shape=[jax.ShapeDtypeStruct((BLK, FB), BF16),...  174 us
    unnamed x6, local copies, waits for them, and re-layouts  8.77 us

profile of v1, /device:TPU:39, one launch (start us, length us, event | category | flops | bytes accessed | tf_op | source)
XLA Modules:
  0.0 183.3 jit_solution(9767597444465023713)
XLA Ops:
  0.6 173.9 %updown.1 = (bf16[64,3072]{1,0:T(8,128)(2,1)}, bf16[64,768]{1,0:T(8,128)(2,1)}, bf16[768,3072]{1,0:T(8,128)(2,1)}, f32[1,3072]{1,0:T(1,128)}) custom-call(bf16[64,768]{1,0:T(8,128)(2,1)} %tok_in.1, bf16[768,3072]{1,0:T(8,128)(2,1)} %w_in.1, f32[1,3072]{1,0:T(1,128)} %bitcast.3, bf16[64,3072]{1,0:T(8,128)(2,1)} %cot_in.1), custom_call_target="tpu_custom_call" | custom-call | tf_op jit(solution)/shard_map/updown/pallas_call | solution.py:259
  174.5 1.8 copy.12
  176.3 1.5 copy.13
  177.8 0.0 copy-start
  177.8 4.9 %copy.14 = bf16[768,3072]{1,0:T(8,128)(2,1)} copy(bf16[768,3072]{1,0:T(8,128)(2,1)} %get-tuple-element.18) | data formatting | bytes 9437184
  182.7 0.0 copy-done
  182.7 0.6 copy.15
Async XLA Ops:
  177.8 4.9 %copy-start = (f32[1,3072]{1,0:T(1,128)S(1)}, f32[1,3072]{1,0:T(1,128)}, u32[]{:S(2)}) copy-start(f32[1,3072]{1,0:T(1,128)} %get-tuple-element.11) | copy-start | bytes 36868

commit v2 on v0

v2 whole, which is shorter than its diff:
```python
import jax
import jax.numpy as jnp
from jax import lax
from jax.experimental import pallas as pl
from jax.experimental.pallas import tpu as pltpu
from jax.sharding import PartitionSpec as P

MESH = pl.DeviceIdType.MESH
BF16 = jnp.bfloat16
F32 = jnp.float32
TOK, DB, FB, BLK = 1024, 768, 3072, 64
H, C = 4, 3
KINDS = "yyyyyyyyyyyy"
J = H * C
R, W = BLK // H, FB // C
GELU_C = 0.7978845608028654
GELU_A = 0.044715

ORDER = (
    ("F1", 0), ("F2u", 0), ("F2d", 0), ("F5d", 0), ("F1", 1), ("F2u", 1), ("F2d", 1), ("F5d", 1), ("F3u", 0), ("F3d", 0),
    ("F1", 2), ("F2u", 2), ("F2d", 2), ("F5d", 2), ("F3u", 1), ("F3d", 1), ("F5A", 0), ("F5B", 0), ("A", 1), ("F1", 3),
    ("F2u", 3), ("F2d", 3), ("F5d", 3), ("F3u", 2), ("F3d", 2), ("F5A", 1), ("F5B", 1), ("F1", 4), ("F2u", 4), ("F2d", 4),
    ("F5d", 4), ("F3u", 3), ("F3d", 3), ("F5A", 2), ("F5B", 2), ("A", 2), ("F1", 5), ("F2u", 5), ("F2d", 5), ("F5d", 5),
    ("F3u", 4), ("F3d", 4), ("F5A", 3), ("F5B", 3), ("F1", 6), ("F2u", 6), ("F2d", 6), ("F5d", 6), ("F3u", 5), ("F3d", 5),
    ("F5A", 4), ("F5B", 4), ("F1", 7), ("F2u", 7), ("F2d", 7), ("F5d", 7), ("F3u", 6), ("F3d", 6), ("F5A", 5), ("F5B", 5),
    ("A", 3), ("F6", 0), ("F1", 8), ("F2u", 8), ("F2d", 8), ("F5d", 8), ("F3u", 7), ("F3d", 7), ("F5A", 6), ("F5B", 6), ("F6", 1),
    ("F1", 9), ("F2u", 9), ("F2d", 9), ("F5d", 9), ("F3u", 8), ("F3d", 8), ("F5A", 7), ("F5B", 7), ("F6", 2), ("F1", 10),
    ("F2u", 10), ("F2d", 10), ("F5d", 10), ("F3u", 9), ("F3d", 9), ("F5A", 8), ("F5B", 8), ("F6", 3), ("F1", 11), ("F2u", 11),
    ("F2d", 11), ("F5d", 11), ("F3u", 10), ("F3d", 10), ("F5A", 9), ("F5B", 9), ("TT", 0), ("F6", 4), ("F7", 0, 0), ("F3u", 11),
    ("F3d", 11), ("F5A", 10), ("F5B", 10), ("F7", 0, 1), ("F7", 0, 3), ("F7", 0, 2), ("F6", 5), ("F7", 1, 0), ("F8", 0, 0),
    ("F5A", 11), ("F5B", 11), ("F8", 0, 3), ("F7", 1, 1), ("F7", 1, 3), ("F8", 0, 1), ("F7", 1, 2), ("F8", 0, 2), ("F6", 6),
    ("F7", 2, 0), ("F8", 1, 0), ("F8", 1, 3), ("F7", 2, 1), ("F7", 2, 3), ("F8", 1, 1), ("F7", 2, 2), ("F8", 1, 2), ("F6", 7),
    ("F9t", 0), ("F7", 3, 0), ("F8", 2, 0), ("F8", 2, 3), ("F7", 3, 1), ("F7", 3, 3), ("F8", 2, 1), ("F7", 3, 2), ("F8", 2, 2),
    ("F6", 8), ("F9t", 1), ("F7", 4, 0), ("F8", 3, 0), ("F8", 3, 3), ("F7", 4, 1), ("F7", 4, 3), ("F8", 3, 1), ("F7", 4, 2),
    ("F8", 3, 2), ("F6", 9), ("F9t", 2), ("T1", 0), ("F7", 5, 0), ("F8", 4, 0), ("F8", 4, 3), ("F7", 5, 1), ("F7", 5, 3),
    ("F7", 5, 2), ("F8", 4, 1), ("F8", 4, 2), ("F6", 10), ("F9t", 3), ("F7", 6, 0), ("F8", 5, 0), ("F8", 5, 3), ("F7", 6, 1),
    ("F7", 6, 3), ("F7", 6, 2), ("F8", 5, 1), ("F8", 5, 2), ("F6", 11), ("F9t", 4), ("F7", 7, 0), ("F8", 6, 0), ("F8", 6, 3),
    ("F7", 7, 1), ("F7", 7, 3), ("F7", 7, 2), ("F8", 6, 1), ("F8", 6, 2), ("F9t", 5), ("T2", 0), ("T1", 1), ("F7", 8, 0),
    ("F8", 7, 0), ("F8", 7, 3), ("F7", 8, 1), ("F7", 8, 3), ("F7", 8, 2), ("F8", 7, 1), ("F8", 7, 2), ("F9t", 6), ("F7", 9, 0),
    ("F8", 8, 0), ("F8", 8, 3), ("F7", 9, 1), ("F7", 9, 3), ("F7", 9, 2), ("F8", 8, 1), ("F8", 8, 2), ("F9t", 7), ("F7", 10, 0),
    ("F8", 9, 0), ("F8", 9, 3), ("F7", 10, 1), ("F7", 10, 3), ("F7", 10, 2), ("F8", 9, 1), ("F8", 9, 2), ("F9t", 8), ("T2", 1),
    ("T1", 2), ("F7", 11, 0), ("F8", 10, 0), ("F8", 10, 3), ("F7", 11, 1), ("F7", 11, 3), ("F7", 11, 2), ("F8", 10, 1),
    ("F8", 10, 2), ("F9t", 9), ("F8", 11, 0), ("F9g", 0, 0), ("F8", 11, 3), ("F9g", 0, 1), ("F8", 11, 1), ("F9g", 0, 2),
    ("F8", 11, 2), ("F9t", 10), ("F9g", 1, 0), ("F9g", 1, 1), ("F9g", 1, 2), ("F9t", 11), ("T2", 2), ("T1", 3), ("F9g", 2, 0),
    ("T2", 3), ("F9g", 2, 1), ("F9g", 2, 2), ("T3", 0), ("T3", 1), ("T3", 2), ("T3", 3),
)


def kernel(
    tok_in, w_in, b_in, cot_in, act, gto, gw, gb,
    tok, tokt, wv, cot, bias, part, ra, rb, mine, zs, zr, zo, gh, gtacc, gts, gpr, gx, gxr,
    lsem, ssem, rsem,
):
    row, col = lax.axis_index("row"), lax.axis_index("col")
    y, zh = row // 4, row % 4
    q, core = col // 2, col % 2
    other = 1 - core

    groups, used = {}, {"r": 0, "l": 0}

    def remote(src, dst, device, *group):
        i = used["r"]
        used["r"] += 1
        copy = pltpu.make_async_remote_copy(
            src_ref=src, dst_ref=dst, send_sem=ssem.at[groups.setdefault(group, len(groups))], recv_sem=rsem.at[i],
            device_id=device, device_id_type=MESH,
        )
        copy.start()
        return copy

    def drain(ref, *group):
        pltpu.make_async_remote_copy(
            src_ref=ref, dst_ref=ref, send_sem=ssem.at[groups[group]], recv_sem=rsem.at[0], device_id=partner, device_id_type=MESH
        ).wait_send()

    def local(src, dst):
        i = used["l"]
        used["l"] += 1
        copy = pltpu.make_async_copy(src, dst, lsem.at[i])
        copy.start()
        return copy

    partner = (row, q * 2 + other)

    def chip(d):
        return lax.rem(q + d, 8)

    own_tok = local(tok_in, tok.at[col // 4, col % 4])
    w_loads = [local(w_in.at[:, pl.ds(c * W, W)], wv.at[c]) for c in range(C)]
    cot_load = local(cot_in, cot)
    bias_load = local(b_in, bias)

    barrier = pltpu.get_barrier_semaphore()
    peers = [(lax.rem(row + 4 * d, 16), col) for d in (1, 2, 3)]
    peers += [(y * 4 + lax.rem(zh + d, 4), col) for d in (1, 2, 3)]
    peers += [(row, chip(d) * 2 + core) for d in range(1, 8)] + [partner]
    for peer in peers:
        pl.semaphore_signal(barrier, inc=1, device_id=peer, device_id_type=MESH)
    pl.semaphore_wait(barrier, len(peers))

    done = {}

    def send_tokens(h):
        rows = pl.ds(h * R, R)
        mineref = tok.at[col // 4, col % 4, rows]
        done["t", h] = [remote(tok_in.at[rows], mineref, (row, chip(d) * 2 + core), "t", h) for d in (1, 7, 2, 6, 3, 5, 4)]
        done["p", h] = [remote(tok_in.at[rows], mineref, partner, "p", h)]

    send_tokens(0)

    def pass_tokens(h):
        for i, d in enumerate((1, 7, 2, 6, 3, 5, 4)):
            done["t", h][i].wait_recv()
            k = chip(8 - d) * 2 + core
            ref = tok.at[k // 4, k % 4, pl.ds(h * R, R)]
            done["p", h] += [remote(ref, ref, partner, "p", h)]
        if h + 1 < H:
            send_tokens(h + 1)

    def geometry(j):
        return (y, zh, 4, 1) if KINDS[j] == "y" else (zh, y, 1, 4)

    def near(i, d):
        return lax.rem(i + 4 + d, 4)

    def block(j, p, s):
        _, _, pm, sm = geometry(j)
        return p * pm + s * sm

    def ghref(j, p, s):
        k = block(j, p, s)
        return gh.at[j % C, k // 4, k % 4, pl.ds(j // C * R, R)]

    def product(j, p):
        rows = pl.ds(j // C * R, R)
        left = tok[p, :, rows] if KINDS[j] == "y" else tok[:, p, rows]
        return jnp.dot(left.reshape(4 * R, DB), wv[j % C], preferred_element_type=F32).reshape(4, R, W)

    def keep(j, p):
        _, s, _, _ = geometry(j)
        blocks = product(j, p).astype(BF16)
        for t in range(4):
            part[j, p, near(t - s, 3)] = blocks[t]

    def step_a(h):
        pass_tokens(h)

    def f1(j):
        p, s, _, _ = geometry(j)
        h, c = j // C, j % C
        if h == 0:
            w_loads[c].wait()
        if c == 0:
            for copy in done["p", h]:
                copy.wait_recv()
            if h == 0:
                own_tok.wait()
        far = near(p, 2)
        keep(j, far)
        done["a", j] = [
            remote(part.at[j, far, pl.ds(0, 2)], ra.at[j, 0], (block(j, near(p, 1), s), col), "part", j),
            remote(part.at[j, far, pl.ds(2, 2)], ra.at[j, 1], (block(j, near(p, -1), s), col), "part", j),
        ]

    def f2u(j):
        p, s, _, _ = geometry(j)
        up = near(p, 1)
        keep(j, up)
        done["b", j, 0, 1] = remote(part.at[j, up, pl.ds(2, 2)], rb.at[j, 0, pl.ds(2, 2)], (block(j, up, s), col), "part", j)

    def f2d(j):
        p, s, _, _ = geometry(j)
        down = near(p, -1)
        keep(j, down)
        done["b", j, 1, 0] = remote(part.at[j, down, pl.ds(0, 2)], rb.at[j, 1, pl.ds(0, 2)], (block(j, down, s), col), "part", j)

    def f3u(j):
        p, s, _, _ = geometry(j)
        up, half = near(p, 1), pl.ds(0, 2)
        done["a", j][0].wait_recv()
        part[j, up, half] = (part[j, up, half].astype(F32) + ra[j, 0].astype(F32)).astype(BF16)
        done["b", j, 0, 0] = remote(part.at[j, up, half], rb.at[j, 0, half], (block(j, up, s), col), "part", j)

    def f3d(j):
        p, s, _, _ = geometry(j)
        down, half = near(p, -1), pl.ds(2, 2)
        done["a", j][1].wait_recv()
        part[j, down, half] = (part[j, down, half].astype(F32) + ra[j, 1].astype(F32)).astype(BF16)
        done["b", j, 1, 1] = remote(part.at[j, down, half], rb.at[j, 1, half], (block(j, down, s), col), "part", j)

    def f5d(j):
        p, _, _, _ = geometry(j)
        mine[j] = product(j, p)

    def total(j, i):
        _, s, _, _ = geometry(j)
        return mine[j, near(s, i + 1)] + rb[j, 0, i].astype(F32) + rb[j, 1, i].astype(F32)

    def second(j, d):
        p, s, _, _ = geometry(j)
        zs[j, d - 1] = total(j, d - 1).astype(BF16)
        done["z", j, d] = remote(zs.at[j, d - 1], zr.at[j, d - 1], (block(j, p, near(s, d)), col), "zs", j)

    def f5a(j):
        done["b", j, 0, 0].wait_recv()
        done["b", j, 1, 0].wait_recv()
        second(j, 2)
        second(j, 1)

    def f5b(j):
        done["b", j, 0, 1].wait_recv()
        done["b", j, 1, 1].wait_recv()
        second(j, 3)
        zo[j] = total(j, 3)

    def f6(j):
        p, s, _, _ = geometry(j)
        rows, columns = pl.ds(j // C * R, R), pl.ds(j % C * W, W)
        for d in (1, 2, 3):
            done["z", j, d].wait_recv()
        hidden = zo[j] + zr[j, 0].astype(F32) + zr[j, 1].astype(F32) + zr[j, 2].astype(F32) + bias[:, columns]
        square = hidden * hidden
        tanh = jnp.tanh(GELU_C * hidden * (1.0 + GELU_A * square))
        half = 0.5 * (1.0 + tanh)
        slope = half + 0.5 * hidden * (1.0 - tanh * tanh) * (GELU_C * (1.0 + 3.0 * GELU_A * square))
        ref = ghref(j, p, s)
        ref[...] = (cot[rows, columns].astype(F32) * slope).astype(BF16)
        for d in (2, 1, 3):
            done["g", j, d] = remote(ref, ref, (block(j, p, near(s, d)), col), "gz", j)
        act[rows, columns] = (hidden * half).astype(BF16)

    def f7(j, d):
        p, s, _, _ = geometry(j)
        if d > 0:
            done["g", j, d].wait_recv()
        ref = ghref(j, p, near(s, -d))
        done["u", j, d] = remote(ref, ref, (block(j, near(p, 1), s), col), "gy", j)
        done["d", j, d] = remote(ref, ref, (block(j, near(p, -1), s), col), "gy", j)

    def f8(j, d):
        p, s, _, _ = geometry(j)
        if d < 2:
            done["u", j, d].wait_recv()
            ref = ghref(j, near(p, -1), near(s, -d))
            done["f", j, d] = remote(ref, ref, (block(j, near(p, 1), s), col), "gy", j)
        else:
            done["d", j, d].wait_recv()
            ref = ghref(j, near(p, 1), near(s, -d))
            done["f", j, d] = remote(ref, ref, (block(j, near(p, -1), s), col), "gy", j)

    finished = []

    def drain_gather(j):
        rows = pl.ds(j // C * R, R)
        drain(gh.at[j % C, pl.ds(0, 3), :, rows], "gy", j)
        drain(gh.at[j % C, 0, pl.ds(0, 3), rows], "gz", j)

    def f9t(j):
        h, c = j // C, j % C
        first = all(i // C != h for i in finished)
        drain(part.at[j, pl.ds(0, 3)], "part", j)
        drain(zs.at[j], "zs", j)
        if len(finished) >= 2:
            drain_gather(finished[-2])
        finished.append(j)
        for d in range(4):
            done["d" if d < 2 else "u", j, d].wait_recv()
            done["f", j, d].wait_recv()
        left = gh[c, :, :, pl.ds(h * R, R)].reshape(16 * R, W)

        @pl.loop(0, 3)
        def _(i):
            cols = pl.ds(pl.multiple_of(i * 256, 256), 256)
            term = lax.dot_general(left, wv[c, cols], (((1,), (1,)), ((), ())), preferred_element_type=F32).reshape(4, 4, R, 256)
            if first:
                gtacc[h, :, :, :, cols] = term
            else:
                gtacc[h, :, :, :, cols] += term

    def tt(_):
        @pl.loop(0, 4)
        def _(i):
            tokt[:, pl.ds(pl.multiple_of(i * 256, 256), 256)] = tok[i].reshape(4 * BLK, DB).T

    def f9g(c, i):
        columns, rows = pl.ds(c * W, W), pl.ds(i * 256, 256)
        gw[rows, columns] = jnp.dot(tokt[rows], gh[c].reshape(TOK, W), preferred_element_type=F32).astype(BF16)
        if i == 0:
            gb[:, columns] = jnp.sum(gh[c].reshape(TOK, W).astype(F32), axis=0, keepdims=True)

    def t1(h):
        @pl.loop(0, 8)
        def _(i):
            k = i * 2 + other
            gts[h, i] = gtacc[h, k // 4, k % 4].astype(BF16)

        done["pair", h] = remote(gts.at[h], gpr.at[h], partner, "pair", h)

    def t2(h):
        done["pair", h].wait_recv()
        for d in (4, 1, 7, 2, 6, 3, 5):
            i = chip(d)
            k = i * 2 + core
            gx[h, d - 1] = (gtacc[h, k // 4, k % 4] + gpr[h, i].astype(F32)).astype(BF16)
            done["x", h, d] = remote(gx.at[h, d - 1], gxr.at[h, d - 1], (row, k), "x", h)

    def t3(h):
        sum_ = gtacc[h, col // 4, col % 4] + gpr[h, q].astype(F32)
        for d in (1, 7, 2, 6, 3, 5, 4):
            done["x", h, d].wait_recv()
            sum_ += gxr[h, d - 1].astype(F32)
        gto[pl.ds(h * R, R)] = sum_.astype(BF16)

    steps = dict(
        A=step_a, F1=f1, F2u=f2u, F2d=f2d, F3u=f3u, F3d=f3d, F5d=f5d, F5A=f5a, F5B=f5b, F6=f6, F7=f7, F8=f8, F9t=f9t, F9g=f9g,
        TT=tt, T1=t1, T2=t2, T3=t3,
    )
    pass_tokens(0)
    started = False
    for step, *which in ORDER:
        if step == "F6" and not started:
            cot_load.wait()
            bias_load.wait()
            started = True
        steps[step](*which)

    for j in finished[-2:]:
        drain_gather(j)
    for h in range(H):
        drain(gx.at[h], "t", h)
        drain(gts.at[h], "p", h)
        drain(gts.at[h], "pair", h)
        drain(gx.at[h], "x", h)


def deliver(act, gt, gw, gb, act_out, gt_out, gw_out, gb_out, sem):
    pairs = ((gw, gw_out), (act, act_out), (gt, gt_out), (gb, gb_out))
    copies = [pltpu.make_async_copy(a, b, sem.at[i]) for i, (a, b) in enumerate(pairs)]
    for copy in copies:
        copy.start()
    for copy in copies:
        copy.wait()


def on_device(tokens_in, weight_up, bias_up, cotangent):
    anywhere = pl.BlockSpec(memory_space=pl.ANY)
    here = pl.BlockSpec(memory_space=pltpu.VMEM)
    v = pltpu.VMEM
    shapes = [((BLK, FB), BF16), ((BLK, DB), BF16), ((DB, FB), BF16), ((1, FB), F32)]
    results = pl.pallas_call(
        kernel,
        out_shape=[v(*s) for s in shapes],
        in_specs=[anywhere] * 4,
        out_specs=[here] * 4,
        scratch_shapes=[
            v((4, 4, BLK, DB), BF16),
            v((DB, TOK), BF16),
            v((C, DB, W), BF16),
            v((BLK, FB), BF16),
            v((1, FB), F32),
            v((J, 4, 4, R, W), BF16),
            v((J, 2, 2, R, W), BF16),
            v((J, 2, 4, R, W), BF16),
            v((J, 4, R, W), F32),
            v((J, 3, R, W), BF16),
            v((J, 3, R, W), BF16),
            v((J, R, W), F32),
            v((C, 4, 4, BLK, W), BF16),
            v((H, 4, 4, R, DB), F32),
            v((H, 8, R, DB), BF16),
            v((H, 8, R, DB), BF16),
            v((H, 7, R, DB), BF16),
            v((H, 7, R, DB), BF16),
            pltpu.SemaphoreType.DMA((C + 3,)),
            pltpu.SemaphoreType.DMA((4 * J + 4 * H,)),
            pltpu.SemaphoreType.DMA((24 * J + 23 * H,)),
        ],
        compiler_params=pltpu.CompilerParams(collective_id=0, has_side_effects=True, vmem_limit_bytes=58 * 2**20),
        name="updown",
    )(tokens_in, weight_up, bias_up.reshape(1, FB), cotangent)
    act, gt, gw, gb = pl.pallas_call(
        deliver,
        out_shape=[jax.ShapeDtypeStruct(*s) for s in shapes],
        in_specs=[here] * 4,
        out_specs=[anywhere] * 4,
        scratch_shapes=[pltpu.SemaphoreType.DMA((4,))],
        compiler_params=pltpu.CompilerParams(vmem_limit_bytes=2 * 2**20),
        name="deliver",
    )(*[pltpu.with_memory_space_constraint(r, pltpu.VMEM) for r in results])
    return act, gt, gw, gb.reshape(FB)


def solution(mesh):
    return jax.shard_map(
        on_device,
        mesh=mesh,
        in_specs=(P("col", "row"), P("row", "col"), P("col"), P("row", "col")),
        out_specs=(P("row", "col"), P("col", "row"), P("row", "col"), P("col")),
        check_vma=False,
    )
```

time: 346 us -> 144 us (0.42)
  waiting for transfers between devices: 285 us -> 0 us
  Pallas kernels: 0 us -> 142 us
  matrix products: 28.4 us -> 0 us
  between operations: 13.8 us -> 0.8 us
  other arithmetic: 6.83 us -> 0 us
  local copies, waits for them, and re-layouts: 6.64 us -> 0 us
    reduce_scatter x2 -> x0, waiting for transfers between devices: 148 us -> none  [the longest x1 109 us: on_device(): lax.psum_scatter(jnp.dot(block, weight_up, preferred_element_type=jnp.flo...]
    pallas_call x0 -> x2, Pallas kernels: none -> 142 us  [the longest x1 139 us: on_device(): pl.pallas_call(kernel, out_shape=[v(*s) for s in shapes], in_specs=[anywh...]
    all_gather x2 -> x0, waiting for transfers between devices: 137 us -> none  [the longest x1 96.3 us: on_device(): grad_hidden = lax.all_gather(local_grad, 'row', axis=0, tiled=True)]
    dot_general x3 -> x0, matrix products: 28.4 us -> none  [the longest x1 9.82 us: on_device(): lax.dot_general(gathered, grad_hidden, (((0,), (0,)), ((), ())), preferre...]
    unnamed x7 -> x0, local copies, waits for them, and re-layouts: 6.64 us -> none
    reduce_sum x1 -> x0, other arithmetic: 4.32 us -> none  [on_device(): grad_bias = jnp.sum(grad_hidden, axis=0, dtype=jnp.float32)]
  transfers between devices with their start and end apart: 4 -> 0, of which waited for: 4 -> 0; matrix products, arithmetic and copies ran while one was open for 6% -> 0% of each run, Pallas kernels for 0% -> 0%
where the time goes in v2:
time: 144 us; the launch traced here: 143 us
  Pallas kernels  142 us (99%)
    pallas_call x1, Pallas kernels, on_device(): pl.pallas_call(kernel, out_shape=[v(*s) for s in shapes], in_specs=[anywh...  139 us

profile of v2, /device:TPU:2, one launch (start us, length us, event | category | flops | bytes accessed | tf_op | source)
XLA Modules:
  0.0 142.6 jit_solution(4666024943540785036)
XLA Ops:
  0.6 139.4 %updown.1 = (bf16[64,3072]{1,0:T(8,128)(2,1)S(1)}, bf16[64,768]{1,0:T(8,128)(2,1)S(1)}, bf16[768,3072]{1,0:T(8,128)(2,1)S(1)}, f32[1,3072]{1,0:T(1,128)S(1)}) custom-call(bf16[64,768]{1,0:T(8,128)(2,1)} %tok_in.1, bf16[768,3072]{1,0:T(8,128)(2,1)} %w_in.1, f32[1,3072]{1,0:T(1,128)} %bitcast.2, bf16[64,3072]{1,0:T(8,128)(2,1)} %cot_in.1), custom_call_target="tpu_custom_call" | custom-call | tf_op jit(solution)/shard_map/updown/pallas_call | solution.py:350
  140.1 2.4 %deliver.1 = (bf16[64,3072]{1,0:T(8,128)(2,1)}, bf16[64,768]{1,0:T(8,128)(2,1)}, bf16[768,3072]{1,0:T(8,128)(2,1)}, f32[1,3072]{1,0:T(1,128)}) custom-call(bf16[64,3072]{1,0:T(8,128)(2,1)S(1)} %get-tuple-element.12.act, bf16[64,768]{1,0:T(8,128)(2,1)S(1)} %get-tuple-element.13.gt, bf16[768,3072]{1,0:T(8,128)(2,1)S(1)} %get-tuple-element.14.gw, ...), custom_call_target="tpu_custom_call" | custom-call | tf_op jit(solution)/shard_map/deliver/pallas_call | solution.py:381

commit v3 on v2

--- a/solution.py
+++ b/solution.py
@@ -10,45 +10,47 @@
 F32 = jnp.float32
 TOK, DB, FB, BLK = 1024, 768, 3072, 64
 H, C = 4, 3
-KINDS = "yyyyyyyyyyyy"
+KINDS = "yzyyzyyyyyyy"
 J = H * C
 R, W = BLK // H, FB // C
 GELU_C = 0.7978845608028654
 GELU_A = 0.044715
 
 ORDER = (
-    ("F1", 0), ("F2u", 0), ("F2d", 0), ("F5d", 0), ("F1", 1), ("F2u", 1), ("F2d", 1), ("F5d", 1), ("F3u", 0), ("F3d", 0),
-    ("F1", 2), ("F2u", 2), ("F2d", 2), ("F5d", 2), ("F3u", 1), ("F3d", 1), ("F5A", 0), ("F5B", 0), ("A", 1), ("F1", 3),
-    ("F2u", 3), ("F2d", 3), ("F5d", 3), ("F3u", 2), ("F3d", 2), ("F5A", 1), ("F5B", 1), ("F1", 4), ("F2u", 4), ("F2d", 4),
-    ("F5d", 4), ("F3u", 3), ("F3d", 3), ("F5A", 2), ("F5B", 2), ("A", 2), ("F1", 5), ("F2u", 5), ("F2d", 5), ("F5d", 5),
-    ("F3u", 4), ("F3d", 4), ("F5A", 3), ("F5B", 3), ("F1", 6), ("F2u", 6), ("F2d", 6), ("F5d", 6), ("F3u", 5), ("F3d", 5),
-    ("F5A", 4), ("F5B", 4), ("F1", 7), ("F2u", 7), ("F2d", 7), ("F5d", 7), ("F3u", 6), ("F3d", 6), ("F5A", 5), ("F5B", 5),
-    ("A", 3), ("F6", 0), ("F1", 8), ("F2u", 8), ("F2d", 8), ("F5d", 8), ("F3u", 7), ("F3d", 7), ("F5A", 6), ("F5B", 6), ("F6", 1),
-    ("F1", 9), ("F2u", 9), ("F2d", 9), ("F5d", 9), ("F3u", 8), ("F3d", 8), ("F5A", 7), ("F5B", 7), ("F6", 2), ("F1", 10),
-    ("F2u", 10), ("F2d", 10), ("F5d", 10), ("F3u", 9), ("F3d", 9), ("F5A", 8), ("F5B", 8), ("F6", 3), ("F1", 11), ("F2u", 11),
-    ("F2d", 11), ("F5d", 11), ("F3u", 10), ("F3d", 10), ("F5A", 9), ("F5B", 9), ("TT", 0), ("F6", 4), ("F7", 0, 0), ("F3u", 11),
-    ("F3d", 11), ("F5A", 10), ("F5B", 10), ("F7", 0, 1), ("F7", 0, 3), ("F7", 0, 2), ("F6", 5), ("F7", 1, 0), ("F8", 0, 0),
-    ("F5A", 11), ("F5B", 11), ("F8", 0, 3), ("F7", 1, 1), ("F7", 1, 3), ("F8", 0, 1), ("F7", 1, 2), ("F8", 0, 2), ("F6", 6),
-    ("F7", 2, 0), ("F8", 1, 0), ("F8", 1, 3), ("F7", 2, 1), ("F7", 2, 3), ("F8", 1, 1), ("F7", 2, 2), ("F8", 1, 2), ("F6", 7),
-    ("F9t", 0), ("F7", 3, 0), ("F8", 2, 0), ("F8", 2, 3), ("F7", 3, 1), ("F7", 3, 3), ("F8", 2, 1), ("F7", 3, 2), ("F8", 2, 2),
-    ("F6", 8), ("F9t", 1), ("F7", 4, 0), ("F8", 3, 0), ("F8", 3, 3), ("F7", 4, 1), ("F7", 4, 3), ("F8", 3, 1), ("F7", 4, 2),
-    ("F8", 3, 2), ("F6", 9), ("F9t", 2), ("T1", 0), ("F7", 5, 0), ("F8", 4, 0), ("F8", 4, 3), ("F7", 5, 1), ("F7", 5, 3),
-    ("F7", 5, 2), ("F8", 4, 1), ("F8", 4, 2), ("F6", 10), ("F9t", 3), ("F7", 6, 0), ("F8", 5, 0), ("F8", 5, 3), ("F7", 6, 1),
-    ("F7", 6, 3), ("F7", 6, 2), ("F8", 5, 1), ("F8", 5, 2), ("F6", 11), ("F9t", 4), ("F7", 7, 0), ("F8", 6, 0), ("F8", 6, 3),
-    ("F7", 7, 1), ("F7", 7, 3), ("F7", 7, 2), ("F8", 6, 1), ("F8", 6, 2), ("F9t", 5), ("T2", 0), ("T1", 1), ("F7", 8, 0),
-    ("F8", 7, 0), ("F8", 7, 3), ("F7", 8, 1), ("F7", 8, 3), ("F7", 8, 2), ("F8", 7, 1), ("F8", 7, 2), ("F9t", 6), ("F7", 9, 0),
-    ("F8", 8, 0), ("F8", 8, 3), ("F7", 9, 1), ("F7", 9, 3), ("F7", 9, 2), ("F8", 8, 1), ("F8", 8, 2), ("F9t", 7), ("F7", 10, 0),
-    ("F8", 9, 0), ("F8", 9, 3), ("F7", 10, 1), ("F7", 10, 3), ("F7", 10, 2), ("F8", 9, 1), ("F8", 9, 2), ("F9t", 8), ("T2", 1),
-    ("T1", 2), ("F7", 11, 0), ("F8", 10, 0), ("F8", 10, 3), ("F7", 11, 1), ("F7", 11, 3), ("F7", 11, 2), ("F8", 10, 1),
-    ("F8", 10, 2), ("F9t", 9), ("F8", 11, 0), ("F9g", 0, 0), ("F8", 11, 3), ("F9g", 0, 1), ("F8", 11, 1), ("F9g", 0, 2),
-    ("F8", 11, 2), ("F9t", 10), ("F9g", 1, 0), ("F9g", 1, 1), ("F9g", 1, 2), ("F9t", 11), ("T2", 2), ("T1", 3), ("F9g", 2, 0),
-    ("T2", 3), ("F9g", 2, 1), ("F9g", 2, 2), ("T3", 0), ("T3", 1), ("T3", 2), ("T3", 3),
+    ("F1", 0), ("F2u", 0), ("F2d", 0), ("F5d", 0), ("A0", 1), ("F1", 1), ("F2u", 1), ("F2d", 1), ("F5d", 1), ("F3u", 0),
+    ("F3d", 0), ("A", 1), ("F1", 2), ("F2u", 2), ("F2d", 2), ("F5d", 2), ("F1", 3), ("F2u", 3), ("F2d", 3), ("A0", 2), ("F5A", 0),
+    ("F5d", 3), ("F3u", 2), ("F3d", 2), ("F1", 4), ("F2u", 4), ("F2d", 4), ("F5d", 4), ("A", 2), ("F3u", 3), ("F3d", 3),
+    ("F5C", 0), ("F1", 5), ("F2u", 5), ("F2d", 5), ("F5A", 2), ("F5d", 5), ("A0", 3), ("F1", 6), ("F3u", 1), ("F3d", 1),
+    ("F2u", 6), ("F2d", 6), ("F5A", 3), ("F5d", 6), ("F3u", 5), ("F3d", 5), ("F5C", 2), ("A", 3), ("F1", 7), ("F2u", 7),
+    ("F2d", 7), ("F5d", 7), ("F3u", 6), ("F3d", 6), ("F6", 0), ("F5C", 3), ("F1", 8), ("F2u", 8), ("F2d", 8), ("F5A", 5),
+    ("F5d", 8), ("F3u", 7), ("F3d", 7), ("F1", 9), ("F3u", 4), ("F3d", 4), ("F2u", 9), ("F2d", 9), ("F5A", 6), ("F5d", 9),
+    ("F3u", 8), ("F3d", 8), ("F5A", 1), ("F6", 2), ("F5C", 5), ("F1", 10), ("F2u", 10), ("F2d", 10), ("F5A", 7), ("F5d", 10),
+    ("F3u", 9), ("F3d", 9), ("F6", 3), ("F5C", 6), ("F6R", 0), ("F1", 11), ("F2u", 11), ("F2d", 11), ("F5A", 8), ("F5d", 11),
+    ("F7", 0, 0), ("F3u", 10), ("F3d", 10), ("TT", 0), ("F5C", 7), ("F5A", 9), ("F7", 0, 1), ("F7", 0, 3), ("F7", 0, 2),
+    ("F3u", 11), ("F3d", 11), ("F5A", 4), ("F6", 5), ("F5C", 8), ("F6R", 2), ("F5A", 10), ("F7", 2, 0), ("F6", 6), ("F5C", 9),
+    ("F6R", 3), ("F8", 0, 1), ("F8", 0, 0), ("F8", 0, 2), ("F8", 0, 3), ("F5A", 11), ("F5C", 1), ("F7", 2, 1), ("F7", 2, 3),
+    ("F7", 2, 2), ("F7", 3, 0), ("F6", 7), ("F5C", 10), ("F7", 3, 1), ("F7", 3, 3), ("F7", 3, 2), ("F6", 1), ("F7", 1, 0),
+    ("F6", 8), ("F5C", 11), ("F6R", 5), ("F8", 2, 1), ("F8", 2, 0), ("F8", 2, 2), ("F8", 2, 3), ("F7", 5, 0), ("F9t", 0),
+    ("F6", 9), ("F6R", 6), ("F8", 3, 1), ("F8", 3, 0), ("F8", 3, 2), ("F8", 3, 3), ("F6R", 1), ("F7", 1, 1), ("F7", 1, 3),
+    ("F5C", 4), ("F7", 5, 1), ("F7", 5, 3), ("F7", 5, 2), ("F7", 6, 0), ("F6", 10), ("F6R", 7), ("F7", 6, 1), ("F7", 6, 3),
+    ("F7", 6, 2), ("F7", 7, 0), ("F6", 4), ("F7", 4, 0), ("F7", 1, 2), ("F9t", 2), ("F6", 11), ("F6R", 8), ("F8", 5, 1),
+    ("F8", 5, 0), ("F8", 5, 2), ("F8", 5, 3), ("F7", 7, 1), ("F7", 7, 3), ("F7", 7, 2), ("F7", 8, 0), ("F9t", 3), ("F6R", 9),
+    ("F8", 6, 1), ("F8", 6, 0), ("F8", 1, 0), ("F8", 6, 2), ("F8", 6, 3), ("F8", 1, 3), ("F6R", 4), ("F7", 4, 1), ("F7", 4, 3),
+    ("F7", 8, 1), ("F7", 8, 3), ("F7", 8, 2), ("F7", 9, 0), ("F6R", 10), ("F8", 7, 1), ("F8", 7, 0), ("F8", 7, 2), ("F8", 7, 3),
+    ("F8", 1, 1), ("F7", 9, 1), ("F8", 1, 2), ("F7", 9, 3), ("F9t", 5), ("F7", 9, 2), ("F7", 10, 0), ("F7", 4, 2), ("F6R", 11),
+    ("F8", 8, 1), ("F8", 8, 0), ("F8", 8, 2), ("F8", 8, 3), ("F7", 10, 1), ("F7", 10, 3), ("F9t", 6), ("F7", 10, 2),
+    ("F7", 11, 0), ("F8", 9, 1), ("F8", 9, 0), ("F8", 4, 0), ("F8", 9, 2), ("F8", 9, 3), ("F8", 4, 3), ("F7", 11, 1),
+    ("F7", 11, 3), ("F9t", 7), ("F7", 11, 2), ("F9t", 1), ("T1", 0), ("F8", 10, 1), ("F8", 10, 0), ("F8", 10, 2), ("F8", 10, 3),
+    ("F8", 4, 1), ("F8", 4, 2), ("F9t", 8), ("T1", 2), ("F8", 11, 1), ("F8", 11, 0), ("F8", 11, 2), ("F8", 11, 3), ("F9t", 9),
+    ("F9t", 4), ("T1", 1), ("T2", 0), ("F9t", 10), ("T2", 2), ("F9t", 11), ("T1", 3), ("F9g", 0, 0), ("F9g", 0, 1), ("F9g", 0, 2),
+    ("T2", 1), ("T2Z", 0), ("F9g", 1, 0), ("T2", 3), ("T2Z", 2), ("F9g", 1, 1), ("F9g", 1, 2), ("F9g", 2, 0), ("T2Z", 1),
+    ("F9g", 2, 1), ("F9g", 2, 2), ("T3", 0), ("T3", 1), ("T3", 2), ("T3", 3),
 )
 
 
 def kernel(
     tok_in, w_in, b_in, cot_in, act, gto, gw, gb,
-    tok, tokt, wv, cot, bias, part, ra, rb, mine, zs, zr, zo, gh, gtacc, gts, gpr, gx, gxr,
+    tok, tokt, wv, cot, bias, part, ra, rb, mine, zs, rr, zr, zo, gh, gtacc, gts, gpr, gx, gxr, gsum,
     lsem, ssem, rsem,
 ):
     row, col = lax.axis_index("row"), lax.axis_index("col")
@@ -100,22 +102,51 @@
 
     done = {}
 
+    zl, x = q // 4, q % 4
+    across = (1 - zl) * 4 + x
+
+    def beside(d):
+        return zl * 4 + lax.rem(x + d, 4)
+
     def send_tokens(h):
         rows = pl.ds(h * R, R)
         mineref = tok.at[col // 4, col % 4, rows]
-        done["t", h] = [remote(tok_in.at[rows], mineref, (row, chip(d) * 2 + core), "t", h) for d in (1, 7, 2, 6, 3, 5, 4)]
+        if h == 0:
+            done["t", h] = [remote(tok_in.at[rows], mineref, (row, chip(d) * 2 + core), "t", h) for d in (1, 7, 2, 6, 3, 5, 4)]
+            done["p", h] = [remote(tok_in.at[rows], mineref, partner, "p", h)]
+            return
+        done["t", h] = [remote(tok_in.at[rows], mineref, (row, c * 2 + core), "t", h) for c in (across, beside(1), beside(3), beside(2))]
         done["p", h] = [remote(tok_in.at[rows], mineref, partner, "p", h)]
 
-    send_tokens(0)
+    def tokref(c, h):
+        k = c * 2 + core
+        return tok.at[k // 4, k % 4, pl.ds(h * R, R)]
+
+    def relay_tokens(h):
+        done["t", h][0].wait_recv()
+        ref = tokref(across, h)
+        done["tr", h] = [remote(ref, ref, (row, beside(d) * 2 + core), "t", h) for d in (1, 3, 2)]
+        done["p", h] += [remote(ref, ref, partner, "p", h)]
 
     def pass_tokens(h):
-        for i, d in enumerate((1, 7, 2, 6, 3, 5, 4)):
-            done["t", h][i].wait_recv()
-            k = chip(8 - d) * 2 + core
-            ref = tok.at[k // 4, k % 4, pl.ds(h * R, R)]
-            done["p", h] += [remote(ref, ref, partner, "p", h)]
+        if h == 0:
+            for i, d in enumerate((1, 7, 2, 6, 3, 5, 4)):
+                done["t", h][i].wait_recv()
+                ref = tokref(chip(8 - d), h)
+                done["p", h] += [remote(ref, ref, partner, "p", h)]
+        else:
+            for i, d in enumerate((1, 3, 2)):
+                done["t", h][i + 1].wait_recv()
+                ref = tokref(beside(4 - d), h)
+                done["p", h] += [remote(ref, ref, partner, "p", h)]
+            for i, d in enumerate((1, 3, 2)):
+                done["tr", h][i].wait_recv()
+                ref = tokref((1 - zl) * 4 + lax.rem(x + 4 - d, 4), h)
+                done["p", h] += [remote(ref, ref, partner, "p", h)]
         if h + 1 < H:
             send_tokens(h + 1)
+
+    send_tokens(0)
 
     def geometry(j):
         return (y, zh, 4, 1) if KINDS[j] == "y" else (zh, y, 1, 4)
@@ -141,9 +172,6 @@
         blocks = product(j, p).astype(BF16)
         for t in range(4):
             part[j, p, near(t - s, 3)] = blocks[t]
-
-    def step_a(h):
-        pass_tokens(h)
 
     def f1(j):
         p, s, _, _ = geometry(j)
@@ -196,43 +224,58 @@
         _, s, _, _ = geometry(j)
         return mine[j, near(s, i + 1)] + rb[j, 0, i].astype(F32) + rb[j, 1, i].astype(F32)
 
-    def second(j, d):
-        p, s, _, _ = geometry(j)
-        zs[j, d - 1] = total(j, d - 1).astype(BF16)
-        done["z", j, d] = remote(zs.at[j, d - 1], zr.at[j, d - 1], (block(j, p, near(s, d)), col), "zs", j)
-
     def f5a(j):
+        p, s, _, _ = geometry(j)
         done["b", j, 0, 0].wait_recv()
         done["b", j, 1, 0].wait_recv()
-        second(j, 2)
-        second(j, 1)
-
-    def f5b(j):
+        zs[j, 1] = total(j, 1).astype(BF16)
+        for i, d in enumerate((1, -1)):
+            half = pl.ds(i * (W // 2), W // 2)
+            done["r", j, i] = remote(zs.at[j, 1, :, half], rr.at[j, i], (block(j, p, near(s, d)), col), "zs", j)
+
+    def f5c(j):
+        p, s, _, _ = geometry(j)
         done["b", j, 0, 1].wait_recv()
         done["b", j, 1, 1].wait_recv()
-        second(j, 3)
+        for i, d in enumerate((1, -1)):
+            at = 2 * i
+            done["r", j, i].wait_recv()
+            whole, extra = total(j, at), rr[j, i].astype(F32)
+            left, right = whole[:, : W // 2], whole[:, W // 2 :]
+            left, right = (left + extra, right) if i == 0 else (left, right + extra)
+            zs[j, at, :, pl.ds(0, W // 2)] = left.astype(BF16)
+            zs[j, at, :, pl.ds(W // 2, W // 2)] = right.astype(BF16)
+            done["z", j, i] = remote(zs.at[j, at], zr.at[j, i], (block(j, p, near(s, d)), col), "zs", j)
         zo[j] = total(j, 3)
 
     def f6(j):
         p, s, _, _ = geometry(j)
         rows, columns = pl.ds(j // C * R, R), pl.ds(j % C * W, W)
-        for d in (1, 2, 3):
-            done["z", j, d].wait_recv()
-        hidden = zo[j] + zr[j, 0].astype(F32) + zr[j, 1].astype(F32) + zr[j, 2].astype(F32) + bias[:, columns]
+        for i in (0, 1):
+            done["z", j, i].wait_recv()
+        hidden = zo[j] + zr[j, 0].astype(F32) + zr[j, 1].astype(F32) + bias[:, columns]
         square = hidden * hidden
         tanh = jnp.tanh(GELU_C * hidden * (1.0 + GELU_A * square))
         half = 0.5 * (1.0 + tanh)
         slope = half + 0.5 * hidden * (1.0 - tanh * tanh) * (GELU_C * (1.0 + 3.0 * GELU_A * square))
         ref = ghref(j, p, s)
         ref[...] = (cot[rows, columns].astype(F32) * slope).astype(BF16)
-        for d in (2, 1, 3):
-            done["g", j, d] = remote(ref, ref, (block(j, p, near(s, d)), col), "gz", j)
+        for i, d in enumerate((1, -1)):
+            done["g", j, i] = remote(ref, ref, (block(j, p, near(s, d)), col), "gz", j)
         act[rows, columns] = (hidden * half).astype(BF16)
 
+    def f6r(j):
+        p, s, _, _ = geometry(j)
+        for i, d in enumerate((1, -1)):
+            done["g", j, i].wait_recv()
+            ref = ghref(j, p, near(s, -d)).at[:, pl.ds(i * (W // 2), W // 2)]
+            done["h", j, i] = remote(ref, ref, (block(j, p, near(s, d)), col), "gz", j)
+
     def f7(j, d):
         p, s, _, _ = geometry(j)
-        if d > 0:
-            done["g", j, d].wait_recv()
+        if d == 2:
+            done["h", j, 0].wait_recv()
+            done["h", j, 1].wait_recv()
         ref = ghref(j, p, near(s, -d))
         done["u", j, d] = remote(ref, ref, (block(j, near(p, 1), s), col), "gy", j)
         done["d", j, d] = remote(ref, ref, (block(j, near(p, -1), s), col), "gy", j)
@@ -296,24 +339,49 @@
 
         done["pair", h] = remote(gts.at[h], gpr.at[h], partner, "pair", h)
 
+    def share(h, c):
+        k = c * 2 + core
+        return gtacc[h, k // 4, k % 4] + gpr[h, c].astype(F32)
+
     def t2(h):
         done["pair", h].wait_recv()
-        for d in (4, 1, 7, 2, 6, 3, 5):
-            i = chip(d)
-            k = i * 2 + core
-            gx[h, d - 1] = (gtacc[h, k // 4, k % 4] + gpr[h, i].astype(F32)).astype(BF16)
-            done["x", h, d] = remote(gx.at[h, d - 1], gxr.at[h, d - 1], (row, k), "x", h)
+        if h == H - 1:
+            for d in (4, 1, 7, 2, 6, 3, 5):
+                c = chip(d)
+                gx[h, d - 1] = share(h, c).astype(BF16)
+                done["x", h, d] = remote(gx.at[h, d - 1], gxr.at[h, d - 1], (row, c * 2 + core), "x", h)
+            return
+        for d in (2, 1, 3):
+            at = 2 * (d - 1)
+            gx[h, at] = share(h, beside(d)).astype(BF16)
+            gx[h, at + 1] = share(h, (1 - zl) * 4 + lax.rem(x + d, 4)).astype(BF16)
+            two = pl.ds(at, 2)
+            done["x", h, d] = remote(gx.at[h, two], gxr.at[h, two], (row, beside(d) * 2 + core), "x", h)
+
+    def t2z(h):
+        own, far = share(h, q), share(h, across)
+        for d in (1, 3, 2):
+            done["x", h, d].wait_recv()
+            own += gxr[h, 2 * (d - 1)].astype(F32)
+            far += gxr[h, 2 * (d - 1) + 1].astype(F32)
+        gsum[h] = own
+        gx[h, 6] = far.astype(BF16)
+        done["xz", h] = remote(gx.at[h, 6], gxr.at[h, 6], (row, across * 2 + core), "x", h)
 
     def t3(h):
-        sum_ = gtacc[h, col // 4, col % 4] + gpr[h, q].astype(F32)
-        for d in (1, 7, 2, 6, 3, 5, 4):
-            done["x", h, d].wait_recv()
-            sum_ += gxr[h, d - 1].astype(F32)
+        if h == H - 1:
+            sum_ = share(h, q)
+            for d in (1, 7, 2, 6, 3, 5, 4):
+                done["x", h, d].wait_recv()
+                sum_ += gxr[h, d - 1].astype(F32)
+        else:
+            done["xz", h].wait_recv()
+            sum_ = gsum[h] + gxr[h, 6].astype(F32)
         gto[pl.ds(h * R, R)] = sum_.astype(BF16)
 
     steps = dict(
-        A=step_a, F1=f1, F2u=f2u, F2d=f2d, F3u=f3u, F3d=f3d, F5d=f5d, F5A=f5a, F5B=f5b, F6=f6, F7=f7, F8=f8, F9t=f9t, F9g=f9g,
-        TT=tt, T1=t1, T2=t2, T3=t3,
+        A0=relay_tokens, A=pass_tokens, F1=f1, F2u=f2u, F2d=f2d, F3u=f3u, F3d=f3d, F5d=f5d, F5A=f5a, F5C=f5c, F6=f6, F6R=f6r, F7=f7, F8=f8, F9t=f9t, F9g=f9g,
+        TT=tt, T1=t1, T2=t2, T2Z=t2z, T3=t3,
     )
     pass_tokens(0)
     started = False
@@ -363,7 +431,8 @@
             v((J, 2, 4, R, W), BF16),
             v((J, 4, R, W), F32),
             v((J, 3, R, W), BF16),
-            v((J, 3, R, W), BF16),
+            v((J, 2, R, W // 2), BF16),
+            v((J, 2, R, W), BF16),
             v((J, R, W), F32),
             v((C, 4, 4, BLK, W), BF16),
             v((H, 4, 4, R, DB), F32),
@@ -371,9 +440,10 @@
             v((H, 8, R, DB), BF16),
             v((H, 7, R, DB), BF16),
             v((H, 7, R, DB), BF16),
+            v((H - 1, R, DB), F32),
             pltpu.SemaphoreType.DMA((C + 3,)),
             pltpu.SemaphoreType.DMA((4 * J + 4 * H,)),
-            pltpu.SemaphoreType.DMA((24 * J + 23 * H,)),
+            pltpu.SemaphoreType.DMA((26 * J + 23 * H,)),
         ],
         compiler_params=pltpu.CompilerParams(collective_id=0, has_side_effects=True, vmem_limit_bytes=58 * 2**20),
         name="updown",

time: 144 us -> 131 us (0.910)
  Pallas kernels: 142 us -> 129 us
    pallas_call x1, Pallas kernels: 139 us -> 127 us  [on_device(): pl.pallas_call(kernel, out_shape=[v(*s) for s in shapes], in_specs=[anywh...]
where the time goes in v3:
time: 131 us; the launch traced here: 130 us
  Pallas kernels  129 us (98%)
    pallas_call x1, Pallas kernels, on_device(): pl.pallas_call(kernel, out_shape=[v(*s) for s in shapes], in_specs=[anywh...  127 us

profile of v3, /device:TPU:2, one launch (start us, length us, event | category | flops | bytes accessed | tf_op | source)
XLA Modules:
  0.0 130.0 jit_solution(13313731127925295943)
XLA Ops:
  0.6 126.9 %updown.1 = (bf16[64,3072]{1,0:T(8,128)(2,1)S(1)}, bf16[64,768]{1,0:T(8,128)(2,1)S(1)}, bf16[768,3072]{1,0:T(8,128)(2,1)S(1)}, f32[1,3072]{1,0:T(1,128)S(1)}) custom-call(bf16[64,768]{1,0:T(8,128)(2,1)} %tok_in.1, bf16[768,3072]{1,0:T(8,128)(2,1)} %w_in.1, f32[1,3072]{1,0:T(1,128)} %bitcast.2, bf16[64,3072]{1,0:T(8,128)(2,1)} %cot_in.1), custom_call_target="tpu_custom_call" | custom-call | tf_op jit(solution)/shard_map/updown/pallas_call | solution.py:418
  127.5 2.4 %deliver.1 = (bf16[64,3072]{1,0:T(8,128)(2,1)}, bf16[64,768]{1,0:T(8,128)(2,1)}, bf16[768,3072]{1,0:T(8,128)(2,1)}, f32[1,3072]{1,0:T(1,128)}) custom-call(bf16[64,3072]{1,0:T(8,128)(2,1)S(1)} %get-tuple-element.12.act, bf16[64,768]{1,0:T(8,128)(2,1)S(1)} %get-tuple-element.13.gt, bf16[768,3072]{1,0:T(8,128)(2,1)S(1)} %get-tuple-element.14.gw, ...), custom_call_target="tpu_custom_call" | custom-call | tf_op jit(solution)/shard_map/deliver/pallas_call | solution.py:451

commit v4 on v3

--- a/solution.py
+++ b/solution.py
@@ -43,8 +43,8 @@
     ("F7", 11, 3), ("F9t", 7), ("F7", 11, 2), ("F9t", 1), ("T1", 0), ("F8", 10, 1), ("F8", 10, 0), ("F8", 10, 2), ("F8", 10, 3),
     ("F8", 4, 1), ("F8", 4, 2), ("F9t", 8), ("T1", 2), ("F8", 11, 1), ("F8", 11, 0), ("F8", 11, 2), ("F8", 11, 3), ("F9t", 9),
     ("F9t", 4), ("T1", 1), ("T2", 0), ("F9t", 10), ("T2", 2), ("F9t", 11), ("T1", 3), ("F9g", 0, 0), ("F9g", 0, 1), ("F9g", 0, 2),
-    ("T2", 1), ("T2Z", 0), ("F9g", 1, 0), ("T2", 3), ("T2Z", 2), ("F9g", 1, 1), ("F9g", 1, 2), ("F9g", 2, 0), ("T2Z", 1),
-    ("F9g", 2, 1), ("F9g", 2, 2), ("T3", 0), ("T3", 1), ("T3", 2), ("T3", 3),
+    ("T2", 1), ("T2Z", 0), ("F9g", 1, 0), ("T2", 3), ("T2Z", 2), ("F9g", 1, 1), ("F9g", 1, 2), ("T2Z", 1), ("F9g", 2, 0),
+    ("F9g", 2, 1), ("F9g", 2, 2), ("T3", 0), ("T3", 2), ("T3", 3), ("T3", 1),
 )
 
 
@@ -58,11 +58,10 @@
     q, core = col // 2, col % 2
     other = 1 - core
 
-    groups, used = {}, {"r": 0, "l": 0}
-
-    def remote(src, dst, device, *group):
-        i = used["r"]
-        used["r"] += 1
+    groups, arrivals, used = {}, {}, {"l": 0}
+
+    def remote(src, dst, device, *group, into=None):
+        i = arrivals.setdefault(into or ("one", len(arrivals)), len(arrivals))
         copy = pltpu.make_async_remote_copy(
             src_ref=src, dst_ref=dst, send_sem=ssem.at[groups.setdefault(group, len(groups))], recv_sem=rsem.at[i],
             device_id=device, device_id_type=MESH,
@@ -74,6 +73,11 @@
         pltpu.make_async_remote_copy(
             src_ref=ref, dst_ref=ref, send_sem=ssem.at[groups[group]], recv_sem=rsem.at[0], device_id=partner, device_id_type=MESH
         ).wait_send()
+
+    def arrived(ref, *into):
+        pltpu.make_async_remote_copy(
+            src_ref=ref, dst_ref=ref, send_sem=ssem.at[0], recv_sem=rsem.at[arrivals[into]], device_id=partner, device_id_type=MESH
+        ).wait_recv()
 
     def local(src, dst):
         i = used["l"]
@@ -113,10 +117,10 @@
         mineref = tok.at[col // 4, col % 4, rows]
         if h == 0:
             done["t", h] = [remote(tok_in.at[rows], mineref, (row, chip(d) * 2 + core), "t", h) for d in (1, 7, 2, 6, 3, 5, 4)]
-            done["p", h] = [remote(tok_in.at[rows], mineref, partner, "p", h)]
+            done["p", h] = [remote(tok_in.at[rows], mineref, partner, "p", h, into=("p", h))]
             return
         done["t", h] = [remote(tok_in.at[rows], mineref, (row, c * 2 + core), "t", h) for c in (across, beside(1), beside(3), beside(2))]
-        done["p", h] = [remote(tok_in.at[rows], mineref, partner, "p", h)]
+        done["p", h] = [remote(tok_in.at[rows], mineref, partner, "p", h, into=("p", h))]
 
     def tokref(c, h):
         k = c * 2 + core
@@ -125,24 +129,24 @@
     def relay_tokens(h):
         done["t", h][0].wait_recv()
         ref = tokref(across, h)
-        done["tr", h] = [remote(ref, ref, (row, beside(d) * 2 + core), "t", h) for d in (1, 3, 2)]
-        done["p", h] += [remote(ref, ref, partner, "p", h)]
+        done["tr", h] = [remote(ref, ref, (row, beside(d) * 2 + core), "t", h, into=("tr", h)) for d in (1, 3, 2)]
+        done["p", h] += [remote(ref, ref, partner, "p", h, into=("p", h))]
 
     def pass_tokens(h):
         if h == 0:
             for i, d in enumerate((1, 7, 2, 6, 3, 5, 4)):
                 done["t", h][i].wait_recv()
                 ref = tokref(chip(8 - d), h)
-                done["p", h] += [remote(ref, ref, partner, "p", h)]
+                done["p", h] += [remote(ref, ref, partner, "p", h, into=("p", h))]
         else:
             for i, d in enumerate((1, 3, 2)):
                 done["t", h][i + 1].wait_recv()
                 ref = tokref(beside(4 - d), h)
-                done["p", h] += [remote(ref, ref, partner, "p", h)]
-            for i, d in enumerate((1, 3, 2)):
-                done["tr", h][i].wait_recv()
+                done["p", h] += [remote(ref, ref, partner, "p", h, into=("p", h))]
+            arrived(gxr.at[h, pl.ds(0, 3)], "tr", h)
+            for d in (1, 3, 2):
                 ref = tokref((1 - zl) * 4 + lax.rem(x + 4 - d, 4), h)
-                done["p", h] += [remote(ref, ref, partner, "p", h)]
+                done["p", h] += [remote(ref, ref, partner, "p", h, into=("p", h))]
         if h + 1 < H:
             send_tokens(h + 1)
 
@@ -179,8 +183,7 @@
         if h == 0:
             w_loads[c].wait()
         if c == 0:
-            for copy in done["p", h]:
-                copy.wait_recv()
+            arrived(gts.at[h], "p", h)
             if h == 0:
                 own_tok.wait()
         far = near(p, 2)
@@ -194,27 +197,27 @@
         p, s, _, _ = geometry(j)
         up = near(p, 1)
         keep(j, up)
-        done["b", j, 0, 1] = remote(part.at[j, up, pl.ds(2, 2)], rb.at[j, 0, pl.ds(2, 2)], (block(j, up, s), col), "part", j)
+        done["b", j, 0, 1] = remote(part.at[j, up, pl.ds(2, 2)], rb.at[j, 0, pl.ds(2, 2)], (block(j, up, s), col), "part", j, into=("b", j, 1))
 
     def f2d(j):
         p, s, _, _ = geometry(j)
         down = near(p, -1)
         keep(j, down)
-        done["b", j, 1, 0] = remote(part.at[j, down, pl.ds(0, 2)], rb.at[j, 1, pl.ds(0, 2)], (block(j, down, s), col), "part", j)
+        done["b", j, 1, 0] = remote(part.at[j, down, pl.ds(0, 2)], rb.at[j, 1, pl.ds(0, 2)], (block(j, down, s), col), "part", j, into=("b", j, 0))
 
     def f3u(j):
         p, s, _, _ = geometry(j)
         up, half = near(p, 1), pl.ds(0, 2)
         done["a", j][0].wait_recv()
         part[j, up, half] = (part[j, up, half].astype(F32) + ra[j, 0].astype(F32)).astype(BF16)
-        done["b", j, 0, 0] = remote(part.at[j, up, half], rb.at[j, 0, half], (block(j, up, s), col), "part", j)
+        done["b", j, 0, 0] = remote(part.at[j, up, half], rb.at[j, 0, half], (block(j, up, s), col), "part", j, into=("b", j, 0))
 
     def f3d(j):
         p, s, _, _ = geometry(j)
         down, half = near(p, -1), pl.ds(2, 2)
         done["a", j][1].wait_recv()
         part[j, down, half] = (part[j, down, half].astype(F32) + ra[j, 1].astype(F32)).astype(BF16)
-        done["b", j, 1, 1] = remote(part.at[j, down, half], rb.at[j, 1, half], (block(j, down, s), col), "part", j)
+        done["b", j, 1, 1] = remote(part.at[j, down, half], rb.at[j, 1, half], (block(j, down, s), col), "part", j, into=("b", j, 1))
 
     def f5d(j):
         p, _, _, _ = geometry(j)
@@ -226,33 +229,30 @@
 
     def f5a(j):
         p, s, _, _ = geometry(j)
-        done["b", j, 0, 0].wait_recv()
-        done["b", j, 1, 0].wait_recv()
+        arrived(rb.at[j, :, pl.ds(0, 2)], "b", j, 0)
         zs[j, 1] = total(j, 1).astype(BF16)
         for i, d in enumerate((1, -1)):
             half = pl.ds(i * (W // 2), W // 2)
-            done["r", j, i] = remote(zs.at[j, 1, :, half], rr.at[j, i], (block(j, p, near(s, d)), col), "zs", j)
+            done["r", j, i] = remote(zs.at[j, 1, :, half], rr.at[j, i], (block(j, p, near(s, d)), col), "zs", j, into=("r", j))
 
     def f5c(j):
         p, s, _, _ = geometry(j)
-        done["b", j, 0, 1].wait_recv()
-        done["b", j, 1, 1].wait_recv()
+        arrived(rb.at[j, :, pl.ds(2, 2)], "b", j, 1)
+        arrived(rr.at[j], "r", j)
         for i, d in enumerate((1, -1)):
             at = 2 * i
-            done["r", j, i].wait_recv()
             whole, extra = total(j, at), rr[j, i].astype(F32)
             left, right = whole[:, : W // 2], whole[:, W // 2 :]
             left, right = (left + extra, right) if i == 0 else (left, right + extra)
             zs[j, at, :, pl.ds(0, W // 2)] = left.astype(BF16)
             zs[j, at, :, pl.ds(W // 2, W // 2)] = right.astype(BF16)
-            done["z", j, i] = remote(zs.at[j, at], zr.at[j, i], (block(j, p, near(s, d)), col), "zs", j)
+            done["z", j, i] = remote(zs.at[j, at], zr.at[j, i], (block(j, p, near(s, d)), col), "zs", j, into=("z", j))
         zo[j] = total(j, 3)
 
     def f6(j):
         p, s, _, _ = geometry(j)
         rows, columns = pl.ds(j // C * R, R), pl.ds(j % C * W, W)
-        for i in (0, 1):
-            done["z", j, i].wait_recv()
+        arrived(zr.at[j], "z", j)
         hidden = zo[j] + zr[j, 0].astype(F32) + zr[j, 1].astype(F32) + bias[:, columns]
         square = hidden * hidden
         tanh = jnp.tanh(GELU_C * hidden * (1.0 + GELU_A * square))
@@ -261,35 +261,35 @@
         ref = ghref(j, p, s)
         ref[...] = (cot[rows, columns].astype(F32) * slope).astype(BF16)
         for i, d in enumerate((1, -1)):
-            done["g", j, i] = remote(ref, ref, (block(j, p, near(s, d)), col), "gz", j)
+            done["g", j, i] = remote(ref, ref, (block(j, p, near(s, d)), col), "gz", j, into=("g", j))
         act[rows, columns] = (hidden * half).astype(BF16)
 
     def f6r(j):
         p, s, _, _ = geometry(j)
+        arrived(gh.at[j % C, 0, pl.ds(0, 2), pl.ds(j // C * R, R)], "g", j)
         for i, d in enumerate((1, -1)):
-            done["g", j, i].wait_recv()
             ref = ghref(j, p, near(s, -d)).at[:, pl.ds(i * (W // 2), W // 2)]
-            done["h", j, i] = remote(ref, ref, (block(j, p, near(s, d)), col), "gz", j)
+            done["h", j, i] = remote(ref, ref, (block(j, p, near(s, d)), col), "gz", j, into=("h", j))
 
     def f7(j, d):
         p, s, _, _ = geometry(j)
         if d == 2:
-            done["h", j, 0].wait_recv()
-            done["h", j, 1].wait_recv()
+            arrived(gh.at[j % C, 0, 0, pl.ds(j // C * R, R)], "h", j)
         ref = ghref(j, p, near(s, -d))
-        done["u", j, d] = remote(ref, ref, (block(j, near(p, 1), s), col), "gy", j)
-        done["d", j, d] = remote(ref, ref, (block(j, near(p, -1), s), col), "gy", j)
+        for key, step in (("u", 1), ("d", -1)):
+            into = None if (key == "u") == (d < 2) else ("rest", j)
+            done[key, j, d] = remote(ref, ref, (block(j, near(p, step), s), col), "gy", j, into=into)
 
     def f8(j, d):
         p, s, _, _ = geometry(j)
         if d < 2:
             done["u", j, d].wait_recv()
             ref = ghref(j, near(p, -1), near(s, -d))
-            done["f", j, d] = remote(ref, ref, (block(j, near(p, 1), s), col), "gy", j)
+            done["f", j, d] = remote(ref, ref, (block(j, near(p, 1), s), col), "gy", j, into=("rest", j))
         else:
             done["d", j, d].wait_recv()
             ref = ghref(j, near(p, 1), near(s, -d))
-            done["f", j, d] = remote(ref, ref, (block(j, near(p, -1), s), col), "gy", j)
+            done["f", j, d] = remote(ref, ref, (block(j, near(p, -1), s), col), "gy", j, into=("rest", j))
 
     finished = []
 
@@ -306,9 +306,7 @@
         if len(finished) >= 2:
             drain_gather(finished[-2])
         finished.append(j)
-        for d in range(4):
-            done["d" if d < 2 else "u", j, d].wait_recv()
-            done["f", j, d].wait_recv()
+        arrived(gh.at[c, pl.ds(0, 2), :, pl.ds(h * R, R)], "rest", j)
         left = gh[c, :, :, pl.ds(h * R, R)].reshape(16 * R, W)
 
         @pl.loop(0, 3)
@@ -349,19 +347,19 @@
             for d in (4, 1, 7, 2, 6, 3, 5):
                 c = chip(d)
                 gx[h, d - 1] = share(h, c).astype(BF16)
-                done["x", h, d] = remote(gx.at[h, d - 1], gxr.at[h, d - 1], (row, c * 2 + core), "x", h)
+                done["x", h, d] = remote(gx.at[h, d - 1], gxr.at[h, d - 1], (row, c * 2 + core), "x", h, into=("x", h))
             return
         for d in (2, 1, 3):
             at = 2 * (d - 1)
             gx[h, at] = share(h, beside(d)).astype(BF16)
             gx[h, at + 1] = share(h, (1 - zl) * 4 + lax.rem(x + d, 4)).astype(BF16)
             two = pl.ds(at, 2)
-            done["x", h, d] = remote(gx.at[h, two], gxr.at[h, two], (row, beside(d) * 2 + core), "x", h)
+            done["x", h, d] = remote(gx.at[h, two], gxr.at[h, two], (row, beside(d) * 2 + core), "x", h, into=("x", h))
 
     def t2z(h):
         own, far = share(h, q), share(h, across)
+        arrived(gxr.at[h, pl.ds(0, 6)], "x", h)
         for d in (1, 3, 2):
-            done["x", h, d].wait_recv()
             own += gxr[h, 2 * (d - 1)].astype(F32)
             far += gxr[h, 2 * (d - 1) + 1].astype(F32)
         gsum[h] = own
@@ -371,8 +369,8 @@
     def t3(h):
         if h == H - 1:
             sum_ = share(h, q)
+            arrived(gxr.at[h], "x", h)
             for d in (1, 7, 2, 6, 3, 5, 4):
-                done["x", h, d].wait_recv()
                 sum_ += gxr[h, d - 1].astype(F32)
         else:
             done["xz", h].wait_recv()
@@ -443,7 +441,7 @@
             v((H - 1, R, DB), F32),
             pltpu.SemaphoreType.DMA((C + 3,)),
             pltpu.SemaphoreType.DMA((4 * J + 4 * H,)),
-            pltpu.SemaphoreType.DMA((26 * J + 23 * H,)),
+            pltpu.SemaphoreType.DMA((13 * J + 12 * H,)),
         ],
         compiler_params=pltpu.CompilerParams(collective_id=0, has_side_effects=True, vmem_limit_bytes=58 * 2**20),
         name="updown",

time: 131 us -> 129 us (0.985)
  no operation moved by 1% of the time
where the time goes in v4:
time: 129 us
  Pallas kernels  128 us (99%)
    pallas_call x1, Pallas kernels, on_device(): pl.pallas_call(kernel, out_shape=[v(*s) for s in shapes], in_specs=[anywh...  126 us

profile of v4, /device:TPU:2, one launch (start us, length us, event | category | flops | bytes accessed | tf_op | source)
XLA Modules:
  0.0 129.1 jit_solution(18027982118925391418)
XLA Ops:
  0.6 125.9 %updown.1 = (bf16[64,3072]{1,0:T(8,128)(2,1)S(1)}, bf16[64,768]{1,0:T(8,128)(2,1)S(1)}, bf16[768,3072]{1,0:T(8,128)(2,1)S(1)}, f32[1,3072]{1,0:T(1,128)S(1)}) custom-call(bf16[64,768]{1,0:T(8,128)(2,1)} %tok_in.1, bf16[768,3072]{1,0:T(8,128)(2,1)} %w_in.1, f32[1,3072]{1,0:T(1,128)} %bitcast.2, bf16[64,3072]{1,0:T(8,128)(2,1)} %cot_in.1), custom_call_target="tpu_custom_call" | custom-call | tf_op jit(solution)/shard_map/updown/pallas_call | solution.py:416
  126.6 2.4 %deliver.1 = (bf16[64,3072]{1,0:T(8,128)(2,1)}, bf16[64,768]{1,0:T(8,128)(2,1)}, bf16[768,3072]{1,0:T(8,128)(2,1)}, f32[1,3072]{1,0:T(1,128)}) custom-call(bf16[64,3072]{1,0:T(8,128)(2,1)S(1)} %get-tuple-element.12.act, bf16[64,768]{1,0:T(8,128)(2,1)S(1)} %get-tuple-element.13.gt, bf16[768,3072]{1,0:T(8,128)(2,1)S(1)} %get-tuple-element.14.gw, ...), custom_call_target="tpu_custom_call" | custom-call | tf_op jit(solution)/shard_map/deliver/pallas_call | solution.py:449

commit v5 on v4

--- a/solution.py
+++ b/solution.py
@@ -42,8 +42,8 @@
     ("F7", 11, 0), ("F8", 9, 1), ("F8", 9, 0), ("F8", 4, 0), ("F8", 9, 2), ("F8", 9, 3), ("F8", 4, 3), ("F7", 11, 1),
     ("F7", 11, 3), ("F9t", 7), ("F7", 11, 2), ("F9t", 1), ("T1", 0), ("F8", 10, 1), ("F8", 10, 0), ("F8", 10, 2), ("F8", 10, 3),
     ("F8", 4, 1), ("F8", 4, 2), ("F9t", 8), ("T1", 2), ("F8", 11, 1), ("F8", 11, 0), ("F8", 11, 2), ("F8", 11, 3), ("F9t", 9),
-    ("F9t", 4), ("T1", 1), ("T2", 0), ("F9t", 10), ("T2", 2), ("F9t", 11), ("T1", 3), ("F9g", 0, 0), ("F9g", 0, 1), ("F9g", 0, 2),
-    ("T2", 1), ("T2Z", 0), ("F9g", 1, 0), ("T2", 3), ("T2Z", 2), ("F9g", 1, 1), ("F9g", 1, 2), ("T2Z", 1), ("F9g", 2, 0),
+    ("F9t", 4), ("T1", 1), ("F9g", 0, 0), ("F9t", 10), ("F9t", 11), ("T1", 3), ("T2", 0), ("F9g", 0, 1), ("T2", 2), ("F9g", 0, 2),
+    ("T2", 1), ("T2Z", 0), ("T2", 3), ("T2Z", 2), ("F9g", 1, 0), ("F9g", 1, 1), ("F9g", 1, 2), ("T2Z", 1), ("F9g", 2, 0),
     ("F9g", 2, 1), ("F9g", 2, 2), ("T3", 0), ("T3", 2), ("T3", 3), ("T3", 1),
 )
 
@@ -189,35 +189,35 @@
         far = near(p, 2)
         keep(j, far)
         done["a", j] = [
-            remote(part.at[j, far, pl.ds(0, 2)], ra.at[j, 0], (block(j, near(p, 1), s), col), "part", j),
-            remote(part.at[j, far, pl.ds(2, 2)], ra.at[j, 1], (block(j, near(p, -1), s), col), "part", j),
+            remote(part.at[j, far, pl.ds(0, 2)], ra.at[j, 0], (block(j, near(p, 1), s), col), "part", j // C),
+            remote(part.at[j, far, pl.ds(2, 2)], ra.at[j, 1], (block(j, near(p, -1), s), col), "part", j // C),
         ]
 
     def f2u(j):
         p, s, _, _ = geometry(j)
         up = near(p, 1)
         keep(j, up)
-        done["b", j, 0, 1] = remote(part.at[j, up, pl.ds(2, 2)], rb.at[j, 0, pl.ds(2, 2)], (block(j, up, s), col), "part", j, into=("b", j, 1))
+        done["b", j, 0, 1] = remote(part.at[j, up, pl.ds(2, 2)], rb.at[j, 0, pl.ds(2, 2)], (block(j, up, s), col), "part", j // C, into=("b", j, 1))
 
     def f2d(j):
         p, s, _, _ = geometry(j)
         down = near(p, -1)
         keep(j, down)
-        done["b", j, 1, 0] = remote(part.at[j, down, pl.ds(0, 2)], rb.at[j, 1, pl.ds(0, 2)], (block(j, down, s), col), "part", j, into=("b", j, 0))
+        done["b", j, 1, 0] = remote(part.at[j, down, pl.ds(0, 2)], rb.at[j, 1, pl.ds(0, 2)], (block(j, down, s), col), "part", j // C, into=("b", j, 0))
 
     def f3u(j):
         p, s, _, _ = geometry(j)
         up, half = near(p, 1), pl.ds(0, 2)
         done["a", j][0].wait_recv()
         part[j, up, half] = (part[j, up, half].astype(F32) + ra[j, 0].astype(F32)).astype(BF16)
-        done["b", j, 0, 0] = remote(part.at[j, up, half], rb.at[j, 0, half], (block(j, up, s), col), "part", j, into=("b", j, 0))
+        done["b", j, 0, 0] = remote(part.at[j, up, half], rb.at[j, 0, half], (block(j, up, s), col), "part", j // C, into=("b", j, 0))
 
     def f3d(j):
         p, s, _, _ = geometry(j)
         down, half = near(p, -1), pl.ds(2, 2)
         done["a", j][1].wait_recv()
         part[j, down, half] = (part[j, down, half].astype(F32) + ra[j, 1].astype(F32)).astype(BF16)
-        done["b", j, 1, 1] = remote(part.at[j, down, half], rb.at[j, 1, half], (block(j, down, s), col), "part", j, into=("b", j, 1))
+        done["b", j, 1, 1] = remote(part.at[j, down, half], rb.at[j, 1, half], (block(j, down, s), col), "part", j // C, into=("b", j, 1))
 
     def f5d(j):
         p, _, _, _ = geometry(j)
@@ -233,7 +233,7 @@
         zs[j, 1] = total(j, 1).astype(BF16)
         for i, d in enumerate((1, -1)):
             half = pl.ds(i * (W // 2), W // 2)
-            done["r", j, i] = remote(zs.at[j, 1, :, half], rr.at[j, i], (block(j, p, near(s, d)), col), "zs", j, into=("r", j))
+            done["r", j, i] = remote(zs.at[j, 1, :, half], rr.at[j, i], (block(j, p, near(s, d)), col), "zs", j // C, into=("r", j))
 
     def f5c(j):
         p, s, _, _ = geometry(j)
@@ -246,7 +246,7 @@
             left, right = (left + extra, right) if i == 0 else (left, right + extra)
             zs[j, at, :, pl.ds(0, W // 2)] = left.astype(BF16)
             zs[j, at, :, pl.ds(W // 2, W // 2)] = right.astype(BF16)
-            done["z", j, i] = remote(zs.at[j, at], zr.at[j, i], (block(j, p, near(s, d)), col), "zs", j, into=("z", j))
+            done["z", j, i] = remote(zs.at[j, at], zr.at[j, i], (block(j, p, near(s, d)), col), "zs", j // C, into=("z", j))
         zo[j] = total(j, 3)
 
     def f6(j):
@@ -261,7 +261,7 @@
         ref = ghref(j, p, s)
         ref[...] = (cot[rows, columns].astype(F32) * slope).astype(BF16)
         for i, d in enumerate((1, -1)):
-            done["g", j, i] = remote(ref, ref, (block(j, p, near(s, d)), col), "gz", j, into=("g", j))
+            done["g", j, i] = remote(ref, ref, (block(j, p, near(s, d)), col), "gz", j // C, into=("g", j))
         act[rows, columns] = (hidden * half).astype(BF16)
 
     def f6r(j):
@@ -269,7 +269,7 @@
         arrived(gh.at[j % C, 0, pl.ds(0, 2), pl.ds(j // C * R, R)], "g", j)
         for i, d in enumerate((1, -1)):
             ref = ghref(j, p, near(s, -d)).at[:, pl.ds(i * (W // 2), W // 2)]
-            done["h", j, i] = remote(ref, ref, (block(j, p, near(s, d)), col), "gz", j, into=("h", j))
+            done["h", j, i] = remote(ref, ref, (block(j, p, near(s, d)), col), "gz", j // C, into=("h", j))
 
     def f7(j, d):
         p, s, _, _ = geometry(j)
@@ -278,34 +278,30 @@
         ref = ghref(j, p, near(s, -d))
         for key, step in (("u", 1), ("d", -1)):
             into = None if (key == "u") == (d < 2) else ("rest", j)
-            done[key, j, d] = remote(ref, ref, (block(j, near(p, step), s), col), "gy", j, into=into)
+            done[key, j, d] = remote(ref, ref, (block(j, near(p, step), s), col), "gy", j // C, into=into)
 
     def f8(j, d):
         p, s, _, _ = geometry(j)
         if d < 2:
             done["u", j, d].wait_recv()
             ref = ghref(j, near(p, -1), near(s, -d))
-            done["f", j, d] = remote(ref, ref, (block(j, near(p, 1), s), col), "gy", j, into=("rest", j))
+            done["f", j, d] = remote(ref, ref, (block(j, near(p, 1), s), col), "gy", j // C, into=("rest", j))
         else:
             done["d", j, d].wait_recv()
             ref = ghref(j, near(p, 1), near(s, -d))
-            done["f", j, d] = remote(ref, ref, (block(j, near(p, -1), s), col), "gy", j, into=("rest", j))
+            done["f", j, d] = remote(ref, ref, (block(j, near(p, -1), s), col), "gy", j // C, into=("rest", j))
 
     finished = []
-
-    def drain_gather(j):
-        rows = pl.ds(j // C * R, R)
-        drain(gh.at[j % C, pl.ds(0, 3), :, rows], "gy", j)
-        drain(gh.at[j % C, 0, pl.ds(0, 3), rows], "gz", j)
 
     def f9t(j):
         h, c = j // C, j % C
         first = all(i // C != h for i in finished)
-        drain(part.at[j, pl.ds(0, 3)], "part", j)
-        drain(zs.at[j], "zs", j)
-        if len(finished) >= 2:
-            drain_gather(finished[-2])
         finished.append(j)
+        if sum(i // C == h for i in finished) == C:
+            drain(part.at[pl.ds(h * C, C), pl.ds(0, 3)], "part", h)
+            drain(zs.at[pl.ds(h * C, C)], "zs", h)
+            drain(gx.at[h], "t", h)
+            drain(gts.at[h], "p", h)
         arrived(gh.at[c, pl.ds(0, 2), :, pl.ds(h * R, R)], "rest", j)
         left = gh[c, :, :, pl.ds(h * R, R)].reshape(16 * R, W)
 
@@ -390,11 +386,10 @@
             started = True
         steps[step](*which)
 
-    for j in finished[-2:]:
-        drain_gather(j)
     for h in range(H):
-        drain(gx.at[h], "t", h)
-        drain(gts.at[h], "p", h)
+        rows = pl.ds(h * R, R)
+        drain(gh.at[:, pl.ds(0, 3), :, rows], "gy", h)
+        drain(gh.at[:, 0, pl.ds(0, 3), rows], "gz", h)
         drain(gts.at[h], "pair", h)
         drain(gx.at[h], "x", h)
 
@@ -440,7 +435,7 @@
             v((H, 7, R, DB), BF16),
             v((H - 1, R, DB), F32),
             pltpu.SemaphoreType.DMA((C + 3,)),
-            pltpu.SemaphoreType.DMA((4 * J + 4 * H,)),
+            pltpu.SemaphoreType.DMA((8 * H,)),
             pltpu.SemaphoreType.DMA((13 * J + 12 * H,)),
         ],
         compiler_params=pltpu.CompilerParams(collective_id=0, has_side_effects=True, vmem_limit_bytes=58 * 2**20),

time: 129 us -> 132 us (1.023)
  Pallas kernels: 128 us -> 131 us
    pallas_call x1, Pallas kernels: 126 us -> 128 us  [on_device(): pl.pallas_call(kernel, out_shape=[v(*s) for s in shapes], in_specs=[anywh...]
where the time goes in v5:
time: 132 us
  Pallas kernels  131 us (99%)
    pallas_call x1, Pallas kernels, on_device(): pl.pallas_call(kernel, out_shape=[v(*s) for s in shapes], in_specs=[anywh...  128 us

profile of v5, /device:TPU:2, one launch (start us, length us, event | category | flops | bytes accessed | tf_op | source)
XLA Modules:
  0.0 131.5 jit_solution(9213528369190206358)
XLA Ops:
  0.6 128.4 %updown.1 = (bf16[64,3072]{1,0:T(8,128)(2,1)S(1)}, bf16[64,768]{1,0:T(8,128)(2,1)S(1)}, bf16[768,3072]{1,0:T(8,128)(2,1)S(1)}, f32[1,3072]{1,0:T(1,128)S(1)}) custom-call(bf16[64,768]{1,0:T(8,128)(2,1)} %tok_in.1, bf16[768,3072]{1,0:T(8,128)(2,1)} %w_in.1, f32[1,3072]{1,0:T(1,128)} %bitcast.2, bf16[64,3072]{1,0:T(8,128)(2,1)} %cot_in.1), custom_call_target="tpu_custom_call" | custom-call | tf_op jit(solution)/shard_map/updown/pallas_call | solution.py:411
  129.0 2.4 %deliver.1 = (bf16[64,3072]{1,0:T(8,128)(2,1)}, bf16[64,768]{1,0:T(8,128)(2,1)}, bf16[768,3072]{1,0:T(8,128)(2,1)}, f32[1,3072]{1,0:T(1,128)}) custom-call(bf16[64,3072]{1,0:T(8,128)(2,1)S(1)} %get-tuple-element.12.act, bf16[64,768]{1,0:T(8,128)(2,1)S(1)} %get-tuple-element.13.gt, bf16[768,3072]{1,0:T(8,128)(2,1)S(1)} %get-tuple-element.14.gw, ...), custom_call_target="tpu_custom_call" | custom-call | tf_op jit(solution)/shard_map/deliver/pallas_call | solution.py:444
